TPU v7x, 32 devices: a whole 2x2x4 slice. The times are simulated.
32 devices in a mesh: dp: 8 (over z, x), row: 2 (over core), col: 2 (over y).
Axes of the slice: x: 2, y: 2, z: 4, core: 2. Of those that a mesh axis runs over, the one named last changes fastest.
Arguments:
- layer_input: bfloat16 [16384, 768], P(('dp', 'row', 'col')), may hold values from -6 to 6
- attn_gain: bfloat16 [768], replicated, may hold values from 0.25 to 1.75
- query_weight: bfloat16 [768, 768], P('row', 'col'), may hold values from -0.21875 to 0.21875
- key_weight: bfloat16 [768, 768], P('row', 'col'), may hold values from -0.21875 to 0.21875
- value_weight: bfloat16 [768, 768], P('row', 'col'), may hold values from -0.21875 to 0.21875
- out_weight: bfloat16 [768, 768], P('col', 'row'), may hold values from -6 to 6
- mlp_gain: bfloat16 [768], replicated, may hold values from 0.25 to 1.75
- act_weight: bfloat16 [768, 1152], P('row', 'col'), may hold values from -0.21875 to 0.21875
- lin_weight: bfloat16 [768, 1152], P('row', 'col'), may hold values from -0.21875 to 0.21875
- down_weight: bfloat16 [1152, 768], P('col', 'row'), may hold values from -0.1875 to 0.1875
- seq_lengths: int32 [8, 2], P('dp'), may hold values from 0 to 2048, as said below
- output_grad: bfloat16 [16384, 768], P(('dp', 'row', 'col')), may hold values from -6 to 6
Outputs:
- layer_output: bfloat16 [16384, 768], P(('dp', 'row', 'col'))
- grad_input: float32 [16384, 768], P(('dp', 'row', 'col'))
- grad_attn_gain: float32 [768], P(('dp', 'row', 'col'))
- grad_query: float32 [768, 768], P(('row', 'dp'), 'col')
- grad_key: float32 [768, 768], P(('row', 'dp'), 'col')
- grad_value: float32 [768, 768], P(('row', 'dp'), 'col')
- grad_out: float32 [768, 768], P('col', ('row', 'dp'))
- grad_mlp_gain: float32 [768], P(('dp', 'row', 'col'))
- grad_act: float32 [768, 1152], P(('row', 'dp'), 'col')
- grad_lin: float32 [768, 1152], P(('row', 'dp'), 'col')
- grad_down: float32 [1152, 768], P('col', ('row', 'dp'))
Inputs may be any that keep to these rules, and one draw needn't show every extreme that they name: `seq_lengths`: row j holds the lengths of the sequences packed one after another from slot 0 of pack j; the nonzero lengths come first and lie between 1024 and 2048, the later ones are 0, and a row sums to at most 2048. In every draw some pack is full and holds a sequence of 2048 tokens, and some other pack holds 2 sequences of 1024 tokens.
All inputs are finite; a program needn't handle non-finite values.
Results may differ from a plain program's by a relative error of at most 0.035.
Values may be sent and summed in bfloat16 or wider, within the bound.
A program may use at most 128 MiB of HBM per device.

v0:
```python
import jax
import jax.numpy as jnp
from jax import lax
from jax.sharding import PartitionSpec as P

D = 768
HEADS = 12


norm_eps = 1e-05
rope_base = 160000.0
masked_score = -1e30


def cut_along(array, dim, length):
    before, after = (array.shape[:dim], array.shape[dim + 1 :])
    return jnp.moveaxis(array.reshape(*before, length, -1, *after), dim, 0)


def sent_and_summed(array, axis, dim):
    pieces = cut_along(array, dim, lax.axis_size(axis))
    arrived = lax.all_to_all(pieces, axis, split_axis=0, concat_axis=0, tiled=True)
    return arrived.astype(jnp.float32).sum(axis=0)


def in_one_piece(arrays, axis, dim, along):
    ends, at = ([], 0)
    for a in arrays[:-1]:
        at += a.shape[along]
        ends.append(at)
    both = jnp.concatenate(arrays, axis=along)
    return tuple(jnp.split(sent_and_summed(both, axis, dim), ends, axis=along))


def matmul(left_side, right_side):
    return jnp.dot(left_side, right_side, preferred_element_type=jnp.float32)


def times_transposed(left_side, right_side):
    return lax.dot_general(
        left_side, right_side, (((1,), (1,)), ((), ())), preferred_element_type=jnp.float32
    )


def transposed_times(left_side, right_side):
    return lax.dot_general(
        left_side, right_side, (((0,), (0,)), ((), ())), preferred_element_type=jnp.float32
    )


def token_layout(lengths, slot_count):
    seq_ends = jnp.cumsum(lengths, dtype=jnp.int32)
    places = jnp.arange(slot_count, dtype=jnp.int32)
    passed = (places[:, None] >= seq_ends[None, :]).astype(jnp.int32)
    segment = jnp.sum(passed, axis=1, dtype=jnp.int32)
    position = places - jnp.sum(passed * lengths[None, :], axis=1, dtype=jnp.int32)
    return (segment, position)


def rope_tables(position, head_dim):
    half_dim = head_dim // 2
    inv_freq = rope_base ** (-2.0 * jnp.arange(half_dim, dtype=jnp.float32) / head_dim)
    angles = position.astype(jnp.float32)[:, None] * inv_freq[None, :]
    return (jnp.cos(angles), jnp.sin(angles))


def rotate(values, cos_tab, sin_tab, direction):
    row_count = values.shape[0]
    half_dim = cos_tab.shape[1]
    paired = values.reshape(row_count, -1, 2, half_dim)
    first_half = paired[:, :, 0, :]
    second_half = paired[:, :, 1, :]
    cos_part = cos_tab[:, None, :]
    sin_part = direction * sin_tab[:, None, :]
    turned = jnp.stack(
        [
            first_half * cos_part - second_half * sin_part,
            second_half * cos_part + first_half * sin_part,
        ],
        axis=2,
    )
    return turned.reshape(row_count, -1)


def norm_forward(stream, gain_vec):
    row_mean = jnp.mean(stream, axis=1, keepdims=True)
    squares = jnp.mean(stream * stream, axis=1, keepdims=True)
    inv_std = lax.rsqrt(squares - row_mean * row_mean + norm_eps)
    normed = (stream - row_mean) * inv_std
    normed_low = (normed * gain_vec.astype(jnp.float32)).astype(jnp.bfloat16)
    return (normed, inv_std, normed_low)


def norm_backward(normed_grad, normed, inv_std, gain_vec):
    scaled = normed_grad * gain_vec.astype(jnp.float32)
    first_mean = jnp.mean(scaled, axis=1, keepdims=True)
    second_mean = jnp.mean(scaled * normed, axis=1, keepdims=True)
    stream_grad = inv_std * (scaled - first_mean - normed * second_mean)
    return (stream_grad, jnp.sum(normed_grad * normed, axis=0))


def half_features(rows_low):
    quarter = rows_low.shape[0]
    width = rows_low.shape[1]
    parts = lax.all_to_all(
        rows_low.reshape(1, 1, quarter, width), "row", split_axis=3, concat_axis=0, tiled=True
    )
    joined = lax.all_gather(parts, "col", axis=1, tiled=True)
    return joined.reshape(4 * quarter, width // 2)


def project_in(normed_low, weight_cat, matrix_count):
    gathered = half_features(normed_low)
    row_count = gathered.shape[0]
    partial_value = matmul(gathered, weight_cat).reshape(row_count, matrix_count, -1)
    summed = lax.psum_scatter(
        partial_value.astype(jnp.bfloat16), "row", scatter_dimension=2, tiled=True
    ).astype(jnp.float32)
    return (summed, gathered)


def project_out(values_low, weight):
    gathered = lax.all_gather(values_low, "row", axis=1, tiled=True)
    product = matmul(gathered, weight)
    quarter = product.shape[0] // 4
    halves = lax.psum_scatter(
        product.reshape(2, 2, quarter, -1).astype(jnp.bfloat16),
        "col",
        scatter_dimension=1,
        tiled=True,
    ).astype(jnp.float32)
    spread = lax.all_to_all(
        halves.astype(jnp.bfloat16), "row", split_axis=0, concat_axis=3, tiled=True
    ).astype(halves.dtype)
    return (spread.reshape(quarter, -1), gathered)


def back_out(branch_grad, weight, gathered_values):
    grad_wide = half_features(branch_grad.astype(jnp.bfloat16))
    weight_grad = transposed_times(gathered_values, grad_wide)
    values_grad = lax.psum_scatter(
        times_transposed(grad_wide, weight).astype(jnp.bfloat16),
        "row",
        scatter_dimension=1,
        tiled=True,
    ).astype(jnp.float32)
    return (values_grad, weight_grad)


def back_in(stacked_grad, weight_cat, gathered_norm):
    grad_wide = lax.all_gather(stacked_grad, "row", axis=2, tiled=True)
    matrix_count = stacked_grad.shape[1]
    weight_view = weight_cat.reshape(weight_cat.shape[0], matrix_count, -1)
    norm_wide = lax.dot_general(
        grad_wide, weight_view, (((1, 2), (1, 2)), ((), ())), preferred_element_type=jnp.float32
    )
    weight_grad = lax.dot_general(
        gathered_norm, grad_wide, (((0,), (0,)), ((), ())), preferred_element_type=jnp.float32
    )
    quarter = norm_wide.shape[0] // 4
    halves = lax.psum_scatter(
        norm_wide.reshape(2, 2, quarter, -1).astype(jnp.bfloat16),
        "col",
        scatter_dimension=1,
        tiled=True,
    ).astype(jnp.float32)
    spread = lax.all_to_all(
        halves.astype(jnp.bfloat16), "row", split_axis=0, concat_axis=3, tiled=True
    ).astype(halves.dtype)
    return (spread.reshape(quarter, -1), weight_grad)


def heads_first(values, head_dim):
    return values.reshape(values.shape[0], -1, head_dim).transpose(1, 0, 2)


def heads_last(values):
    return values.transpose(1, 0, 2).reshape(values.shape[1], -1)


def attend_forward(queries, keys_in, values_in, segment, head_dim):
    row_count = queries.shape[0]
    block_rows = min(512, row_count)
    starts = jnp.arange(row_count // block_rows, dtype=jnp.int32) * block_rows
    score_scale = head_dim ** (-0.5)

    def one_head(operands):
        query_head, key_head, value_head = operands

        def one_block(start_row):
            query_block = lax.dynamic_slice_in_dim(query_head, start_row, block_rows, 0)
            segment_block = lax.dynamic_slice_in_dim(segment, start_row, block_rows, 0)
            scores = times_transposed(query_block, key_head) * score_scale
            scores = jnp.where(segment_block[:, None] == segment[None, :], scores, masked_score)
            row_peak = jnp.max(scores, axis=1, keepdims=True)
            exponent = jnp.exp(scores - row_peak)
            totals = jnp.sum(exponent, axis=1, keepdims=True)
            attn_probs = (exponent / totals).astype(jnp.bfloat16)
            return (matmul(attn_probs, value_head), (row_peak + jnp.log(totals))[:, 0])

        context, log_total = lax.map(one_block, starts)
        return (context.reshape(row_count, head_dim), log_total.reshape(row_count))

    context, log_total = lax.map(
        one_head,
        (
            heads_first(queries, head_dim),
            heads_first(keys_in, head_dim),
            heads_first(values_in, head_dim),
        ),
    )
    return (heads_last(context).astype(jnp.bfloat16), log_total)


def attend_backward(queries, keys_in, values_in, context_grad, log_total, segment, head_dim):
    row_count = queries.shape[0]
    block_rows = min(512, row_count)
    starts = jnp.arange(row_count // block_rows, dtype=jnp.int32) * block_rows
    score_scale = head_dim ** (-0.5)

    def one_head(operands):
        query_head, key_head, value_head, grad_head, total_head = operands

        def one_block(carried, start_row):
            keys_grad, values_grad = carried
            query_block = lax.dynamic_slice_in_dim(query_head, start_row, block_rows, 0)
            grad_block = lax.dynamic_slice_in_dim(grad_head, start_row, block_rows, 0)
            segment_block = lax.dynamic_slice_in_dim(segment, start_row, block_rows, 0)
            total_block = lax.dynamic_slice_in_dim(total_head, start_row, block_rows, 0)
            scores = times_transposed(query_block, key_head) * score_scale
            scores = jnp.where(segment_block[:, None] == segment[None, :], scores, masked_score)
            attn_probs = jnp.exp(scores - total_block[:, None])
            values_grad = values_grad + transposed_times(
                attn_probs.astype(jnp.bfloat16), grad_block
            )
            probs_grad = times_transposed(grad_block, value_head)
            inner_sum = jnp.sum(probs_grad * attn_probs, axis=1, keepdims=True)
            scores_grad = (attn_probs * (probs_grad - inner_sum)).astype(jnp.bfloat16)
            keys_grad = keys_grad + transposed_times(scores_grad, query_block) * score_scale
            return ((keys_grad, values_grad), matmul(scores_grad, key_head) * score_scale)

        zeros_init = jnp.zeros((row_count, head_dim), jnp.float32)
        (keys_grad, values_grad), query_grad = lax.scan(one_block, (zeros_init, zeros_init), starts)
        return (query_grad.reshape(row_count, head_dim), keys_grad, values_grad)

    query_grad, keys_grad, values_grad = lax.map(
        one_head,
        (
            heads_first(queries, head_dim),
            heads_first(keys_in, head_dim),
            heads_first(values_in, head_dim),
            heads_first(context_grad, head_dim),
            log_total,
        ),
    )
    return (heads_last(query_grad), heads_last(keys_grad), heads_last(values_grad))


def geglu(act_in, lin_in):
    return jax.nn.gelu(act_in, approximate=False) * lin_in


def shards(
    layer_input,
    attn_gain,
    query_weight,
    key_weight,
    value_weight,
    out_weight,
    mlp_gain,
    act_weight,
    lin_weight,
    down_weight,
    seq_lengths,
    output_grad,
):
    stream = layer_input.astype(jnp.float32)
    head_dim = D // HEADS
    pack_slots = stream.shape[0] * lax.axis_size("row") * lax.axis_size("col")
    segment, position = token_layout(seq_lengths[0], pack_slots)
    cos_tab, sin_tab = rope_tables(position, head_dim)
    attn_cat = jnp.concatenate((query_weight, key_weight, value_weight), axis=1)
    mlp_cat = jnp.concatenate((act_weight, lin_weight), axis=1)
    normed_attn, inv_attn, low_attn = norm_forward(stream, attn_gain)
    attn_sums, gathered_attn = project_in(low_attn, attn_cat, 3)
    queries = rotate(attn_sums[:, 0], cos_tab, sin_tab, 1.0).astype(jnp.bfloat16)
    keys_in = rotate(attn_sums[:, 1], cos_tab, sin_tab, 1.0).astype(jnp.bfloat16)
    values_in = attn_sums[:, 2].astype(jnp.bfloat16)
    context, log_total = attend_forward(queries, keys_in, values_in, segment, head_dim)
    attn_out, gathered_context = project_out(context, out_weight)
    middle = stream + attn_out
    normed_mlp, inv_mlp, low_mlp = norm_forward(middle, mlp_gain)
    mlp_sums, gathered_mlp = project_in(low_mlp, mlp_cat, 2)
    hidden_full, geglu_pull = jax.vjp(geglu, mlp_sums[:, 0], mlp_sums[:, 1])
    hidden = hidden_full.astype(jnp.bfloat16)
    mlp_out, gathered_hidden = project_out(hidden, down_weight)
    layer_output = (middle + mlp_out).astype(jnp.bfloat16)
    top_grad = output_grad.astype(jnp.float32)
    hidden_grad, grad_down = back_out(top_grad, down_weight, gathered_hidden)
    act_grad, lin_grad = geglu_pull(hidden_grad)
    stacked_mlp = jnp.stack([act_grad, lin_grad], axis=1).astype(jnp.bfloat16)
    mlp_norm_grad, mlp_weight_grad = back_in(stacked_mlp, mlp_cat, gathered_mlp)
    middle_back, gain_mlp_part = norm_backward(mlp_norm_grad, normed_mlp, inv_mlp, mlp_gain)
    middle_grad = top_grad + middle_back
    context_grad, grad_out = back_out(middle_grad, out_weight, gathered_context)
    query_grad, keys_grad, values_grad = attend_backward(
        queries, keys_in, values_in, context_grad.astype(jnp.bfloat16), log_total, segment, head_dim
    )
    stacked_attn = jnp.stack(
        [
            rotate(query_grad, cos_tab, sin_tab, -1.0),
            rotate(keys_grad, cos_tab, sin_tab, -1.0),
            values_grad,
        ],
        axis=1,
    ).astype(jnp.bfloat16)
    attn_norm_grad, attn_weight_grad = back_in(stacked_attn, attn_cat, gathered_attn)
    stream_back, gain_attn_part = norm_backward(attn_norm_grad, normed_attn, inv_attn, attn_gain)
    grad_input = middle_grad + stream_back
    summed = (
        *in_one_piece(
            (
                attn_weight_grad[:, 0].astype(jnp.bfloat16),
                attn_weight_grad[:, 1].astype(jnp.bfloat16),
                attn_weight_grad[:, 2].astype(jnp.bfloat16),
            ),
            "dp",
            0,
            1,
        ),
        sent_and_summed(grad_out.astype(jnp.bfloat16), "dp", 1),
        *in_one_piece(
            (
                mlp_weight_grad[:, 0].astype(jnp.bfloat16),
                mlp_weight_grad[:, 1].astype(jnp.bfloat16),
            ),
            "dp",
            0,
            1,
        ),
        sent_and_summed(grad_down.astype(jnp.bfloat16), "dp", 1),
    )
    gains = (
        lax.psum_scatter(gain_attn_part, ("dp", "row", "col"), scatter_dimension=0, tiled=True),
        lax.psum_scatter(gain_mlp_part, ("dp", "row", "col"), scatter_dimension=0, tiled=True),
    )
    return (
        layer_output,
        grad_input,
        gains[0],
        summed[0],
        summed[1],
        summed[2],
        summed[3],
        gains[1],
        summed[4],
        summed[5],
        summed[6],
    )


def solution(mesh):
    in_specs = (
        P(("dp", "row", "col"), None),
        P(),
        P("row", "col"),
        P("row", "col"),
        P("row", "col"),
        P("col", "row"),
        P(),
        P("row", "col"),
        P("row", "col"),
        P("col", "row"),
        P("dp", None),
        P(("dp", "row", "col"), None),
    )
    out_specs = (
        P(("dp", "row", "col"), None),
        P(("dp", "row", "col"), None),
        P(("dp", "row", "col")),
        P(("row", "dp"), "col"),
        P(("row", "dp"), "col"),
        P(("row", "dp"), "col"),
        P("col", ("row", "dp")),
        P(("dp", "row", "col")),
        P(("row", "dp"), "col"),
        P(("row", "dp"), "col"),
        P("col", ("row", "dp")),
    )
    return jax.shard_map(shards, mesh=mesh, in_specs=in_specs, out_specs=out_specs, check_vma=False)
```

profile of v0, /device:TPU:0, one launch (start us, length us, event | category | flops | bytes accessed | tf_op | source)
XLA Modules:
  0.0 878.8 jit_solution(14070637850889749468)
XLA Ops:
  12.3 5.4 reduce.5
  18.3 4.4 all_to_all.128
  25.7 29.2 %all-gather.21.cloned.1.call-done = bf16[2,2,1,512,384]{4,3,2,0,1:T(8,128)(2,1)} async-done(((bf16[2,1,1,512,384]{4,3,2,0,1:T(8,128)(2,1)}), bf16[2,2,1,512,384]{4,3,2,0,1:T(8,128)(2,1)}) %all-gather.21.cloned.1.call-update) | async-done | bytes 1572880 | tf_op jit(solution)/shard_map/all_gather | solution.py:108
  57.7 4.3 convolution_convert_fusion.1
  66.5 8.2 reduce-scatter.17.cloned.1.call-done
  80.0 2.5 copy.288
  84.0 88.0 %while.64 = (s32[]{:T(128)}, bf16[3,2048,64]{1,2,0:T(8,128)(2,1)}, f32[3,2048]{1,0:T(4,128)S(1)}, bf16[3,2048,64]{2,1,0:T(8,128)(2,1)}, bf16[3,2048,64]{2,1,0:T(...) while((s32[]{:T(128)}, bf16[3,2048,64]{1,2,0:T(8,128)(2,1)}, ...), condition=%wide.region_11.12_spmd.clone.clone, body=%wide.region_6.11_spmd.clone.sunk.clone | while | flops 277872128 | bytes 16845216 | solution.py:204
  87.0 25.0 %while.63 = (s32[]{:T(128)}, bf16[4,512,64]{1,2,0:T(8,128)(2,1)S(1)}, f32[4,512]{1,0:T(4,128)S(1)}, s32[4]{0:T(128)S(1)}, s32[2048]{0:T(1024)S(1)}, /*index=5*/b...) while((s32[]{:T(128)}, ...), condition=%wide.region_10.10_spmd, body=%wide.region_7.9_spmd.sunk | while | flops 277872128 | bytes 13666483 | solution.py:201
  116.4 25.0 %while.63 = (s32[]{:T(128)}, bf16[4,512,64]{1,2,0:T(8,128)(2,1)S(1)}, f32[4,512]{1,0:T(4,128)S(1)}, s32[4]{0:T(128)S(1)}, s32[2048]{0:T(1024)S(1)}, /*index=5*/b...) while((s32[]{:T(128)}, ...), condition=%wide.region_10.10_spmd, body=%wide.region_7.9_spmd.sunk | while | flops 277872128 | bytes 13666483 | solution.py:201
  145.7 25.0 %while.63 = (s32[]{:T(128)}, bf16[4,512,64]{1,2,0:T(8,128)(2,1)S(1)}, f32[4,512]{1,0:T(4,128)S(1)}, s32[4]{0:T(128)S(1)}, s32[2048]{0:T(1024)S(1)}, /*index=5*/b...) while((s32[]{:T(128)}, ...), condition=%wide.region_10.10_spmd, body=%wide.region_7.9_spmd.sunk | while | flops 277872128 | bytes 13666483 | solution.py:201
  172.1 11.0 %all-gather.13.cloned.1.call-done = bf16[2048,384]{0,1:T(8,128)(2,1)} async-done(((bf16[2048,192]{0,1:T(8,128)(2,1)}), bf16[2048,384]{0,1:T(8,128)(2,1)}) %all-gather.13.cloned.1.call-update) | async-done | bytes 1572880 | tf_op jit(solution)/shard_map/all_gather | solution.py:123
  183.1 3.7 convolution_convert_fusion.5
  187.6 52.1 %all-reduce.12.cloned.1.call-done = bf16[2,2,512,384]{3,2,1,0:T(8,128)(2,1)} async-done(((bf16[2,2,512,384]{3,2,1,0:T(8,128)(2,1)}), bf16[2,2,512,384]{3,2,1,0:T(8,128)(2,1)}) %all-reduce.12.cloned.1.call-update) | async-done | bytes 1572880
  241.6 4.9 all_to_all.129
  252.6 6.4 reduce.6
  260.3 5.4 all_to_all.130
  267.3 2.5 copy.342
  272.5 2.9 copy.296
  275.4 6.4 reduce.4
  283.2 5.4 all_to_all.131
  294.8 4.8 all-gather.23.cloned.1.call-done
  302.3 5.5 convolution_convert_fusion
  307.9 20.9 %all-gather.25.cloned.1.call-done = bf16[2,2,1,512,384]{4,3,2,0,1:T(8,128)(2,1)} async-done(((bf16[2,1,1,512,384]{4,3,2,0,1:T(8,128)(2,1)}), bf16[2,2,1,512,384]{4,3,2,0,1:T(8,128)(2,1)}) %all-gather.25.cloned.1.call-update) | async-done | bytes 1572880 | tf_op jit(solution)/shard_map/all_gather | solution.py:108
  331.6 2.9 convolution_convert_fusion.2
  334.6 9.2 %reduce-scatter.19.cloned.1.call-done = bf16[2048,2,288]{0,2,1:T(8,128)(2,1)} async-done(((bf16[2048,2,576]{0,2,1:T(8,128)(2,1)}), bf16[2048,2,288]{0,2,1:T(8,128)(2,1)}) %reduce-scatter.19.cloned.1.call-update) | async-done | bytes 2359312 | tf_op jit(solution)/shard_map/reduce_scatter | solution.py:116
  343.8 4.4 convert_element_type.259
  348.2 9.0 %reduce-scatter.21.cloned.1.call-done = bf16[2048,288]{0,1:T(8,128)(2,1)} async-done(((bf16[2048,576]{0,1:T(8,128)(2,1)}), bf16[2048,288]{0,1:T(8,128)(2,1)}) %reduce-scatter.21.cloned.1.call-update) | async-done | bytes 1179664 | tf_op jit(solution)/shard_map/reduce_scatter | solution.py:141
  357.2 7.1 fusion.74
  368.5 15.3 %all-gather.17.cloned.1.call-done = bf16[2048,2,576]{0,2,1:T(8,128)(2,1)} async-done(((bf16[2048,2,288]{0,2,1:T(8,128)(2,1)}), bf16[2048,2,576]{0,2,1:T(8,128)(2,1)}) %all-gather.17.cloned.1.call-update) | async-done | bytes 4718608 | tf_op jit(solution)/shard_map/all_gather | solution.py:151
  383.8 8.8 %dot_general.78 = bf16[2,2,512,2,576]{2,1,0,4,3:T(2,128)(2,1)} reshape(bf16[2048,2,576]{0,2,1:T(8,128)(2,1)} %all-gather.17.cloned.1.call-done) | data formatting | bytes 9437184 | tf_op jit(solution)/shard_map/dot_general | solution.py:154
  392.6 6.7 bitcast_convert_fusion.1
  400.8 51.3 %all-reduce.14.cloned.1.call-done = bf16[2,2,512,384]{3,2,1,0:T(8,128)(2,1)} async-done(((bf16[2,2,512,384]{3,2,1,0:T(8,128)(2,1)}), bf16[2,2,512,384]{3,2,1,0:T(8,128)(2,1)}) %all-reduce.14.cloned.1.call-update) | async-done | bytes 1572880
  452.1 2.7 constant_dynamic-slice_fusion.2
  457.2 5.4 all_to_all.132
  466.1 5.4 reduce.7
  472.2 4.4 all_to_all.133
  478.7 27.3 %all-gather.27.cloned.1.call-done = bf16[2,2,1,512,384]{4,3,2,0,1:T(8,128)(2,1)} async-done(((bf16[2,1,1,512,384]{4,3,2,0,1:T(8,128)(2,1)}), bf16[2,2,1,512,384]{4,3,2,0,1:T(8,128)(2,1)}) %all-gather.27.cloned.1.call-update) | async-done | bytes 1572880 | tf_op jit(solution)/shard_map/all_gather | solution.py:108
  511.9 8.2 reduce-scatter.23.cloned.1.call-done
  520.2 2.5 copy.305
  524.0 139.2 %while.66 = (s32[]{:T(128)}, f32[3,2048,64]{1,2,0:T(8,128)}, f32[3,2048,64]{1,2,0:T(8,128)}, bf16[3,2048,64]{1,2,0:T(8,128)(2,1)}, bf16[3,2048,64]{2,1,0:T(8,128...) while((s32[]{:T(128)}, f32[3,2048,64]{1,2,0:T(8,128)}, ...), condition=%wide.region_26.27_spmd.clone.clone, body=%wide.region_22.26_spmd.clone.sunk.clone | while | flops 682262016 | bytes 42639880 | solution.py:246
  529.2 37.7 %while.65 = (s32[]{:T(128)}, f32[2048,64]{0,1:T(8,128)S(1)}, f32[2048,64]{0,1:T(8,128)S(1)}, f32[4,512,64]{1,2,0:T(8,128)}, s32[4]{0:T(128)S(1)}, /*index=5*/s32...) while((s32[]{:T(128)}, f32[2048,64]{0,1:T(8,128)S(1)}, ...), condition=%wide.region_25.25_spmd.clone, body=%wide.region_23.24_spmd.clone.sunk | while | flops 682262016 | bytes 35283168 | solution.py:243
  575.6 37.7 %while.65 = (s32[]{:T(128)}, f32[2048,64]{0,1:T(8,128)S(1)}, f32[2048,64]{0,1:T(8,128)S(1)}, f32[4,512,64]{1,2,0:T(8,128)}, s32[4]{0:T(128)S(1)}, /*index=5*/s32...) while((s32[]{:T(128)}, f32[2048,64]{0,1:T(8,128)S(1)}, ...), condition=%wide.region_25.25_spmd.clone, body=%wide.region_23.24_spmd.clone.sunk | while | flops 682262016 | bytes 35283168 | solution.py:243
  622.0 37.7 %while.65 = (s32[]{:T(128)}, f32[2048,64]{0,1:T(8,128)S(1)}, f32[2048,64]{0,1:T(8,128)S(1)}, f32[4,512,64]{1,2,0:T(8,128)}, s32[4]{0:T(128)S(1)}, /*index=5*/s32...) while((s32[]{:T(128)}, f32[2048,64]{0,1:T(8,128)S(1)}, ...), condition=%wide.region_25.25_spmd.clone, body=%wide.region_23.24_spmd.clone.sunk | while | flops 682262016 | bytes 35283168 | solution.py:243
  669.8 3.0 convolution_convert_fusion.8
  673.9 5.8 all-to-all-start.11
  679.7 5.7 convolution_convert_fusion.6
  687.2 6.7 all-to-all-done.11
  693.9 3.6 all-to-all-start.10
  697.8 4.5 convolution_convert_fusion.3
  702.3 6.7 copy.311
  709.0 5.1 fusion.23
  716.8 3.3 convolution_convert_fusion.9
  720.1 4.8 convolution_convert_fusion.7
  724.9 6.0 all-to-all-start.9
  732.1 7.9 all-to-all-done.9
  739.9 3.6 all-to-all-start.8
  745.8 19.6 %all-to-all-done.8 = bf16[8,48,1152]{2,1,0:T(8,128)(2,1)S(1)} async-done(((bf16[8,48,1152]{2,1,0:T(8,128)(2,1)}), bf16[8,48,1152]{2,1,0:T(8,128)(2,1)S(1)}, u32[]{:S(2)}, u32[]{:S(2)}) %all-to-all-start.8) | async-done | bytes 884768 | tf_op jit(solution)/shard_map/all_to_all | solution.py:22
  766.2 36.7 %all-reduce.16.cloned.1.call-done = (bf16[2,2,512,384]{3,2,1,0:T(8,128)(2,1)}, bf16[2,2,512,384]{3,2,1,0:T(8,128)(2,1)}) async-done(((bf16[2,2,512,384]{3,2,1,0:T(8,128)(2,1)}, bf16[2,2,512,384]{3,2,1,0:T(8,128)(2,1)}), (bf16[2,2,512,384]{3,2,1,0:T(8,128)(2,1)}, bf16[2,2,512,384]{3,2,1,0:T(8,128)(2,1)})) %all-reduce.16.cloned.1.call-update) | async-done | bytes 3145744
  805.7 5.3 all_to_all.134
  813.4 39.4 %all-reduce.6 = (f32[768]{0:T(1024)S(1)}, f32[768]{0:T(1024)S(1)}) all-reduce(f32[768]{0:T(1024)S(1)} %get-tuple-element.518, f32[768]{0:T(1024)S(1)} %copy-done.51), channel_id=14, replica_groups=mesh['dp'=8,'row'=2,'col'=2] {'dp','row','col'}, use_global_device_ids=true, to_apply=%region_31.32.clone | all-reduce | flops 1536 | bytes 12288
  854.0 4.6 all_to_all.135
  859.9 3.2 copy.294
  863.1 4.6 fusion.59
  867.7 3.1 copy.319
  (506 shorter events, 275.9 us)
Async XLA Ops:
  7.2 324.5 %copy-start = (bf16[576,384]{1,0:T(8,128)(2,1)S(1)}, bf16[576,384]{1,0:T(8,128)(2,1)}, u32[]{:S(2)}) copy-start(bf16[576,384]{1,0:T(8,128)(2,1)} %param.29) | copy-start | bytes 1327108
  7.2 47.7 %all-gather.21.cloned.1.call-start = ((), (), s32[]{:S(2)}) async-start(), calls=%async_computation.24 | async-start | bytes 2359296 | tf_op jit(solution)/shard_map/all_gather | solution.py:108
  8.0 1.7 copy-start.37
  9.4 2.4 copy-start.5
  23.6 1.3 copy-start.32
  23.6 1.5 copy-start.33
  23.7 1.7 copy-start.34
  24.8 49.9 %reduce-scatter.17.cloned.1.call-start = ((), (), s32[]{:S(2)}) async-start(), calls=%async_computation.16 | async-start | bytes 7077888 | tf_op jit(solution)/shard_map/reduce_scatter | solution.py:116
  25.7 36.3 %copy-start.26 = (bf16[384,1152]{0,1:T(8,128)(2,1)}, bf16[384,1152]{0,1:T(8,128)(2,1)S(1)}, u32[]{:S(2)}) copy-start(bf16[384,1152]{0,1:T(8,128)(2,1)S(1)} %pad_maximum_fusion.2) | copy-start | bytes 2654212
  62.0 121.2 %all-gather.13.cloned.1.call-start = ((), (), s32[]{:S(2)}) async-start(), calls=%async_computation.17 | async-start | bytes 2359296 | tf_op jit(solution)/shard_map/all_gather | solution.py:123
  66.5 11.9 %copy-start.18 = (f32[2048,32]{0,1:T(8,128)}, f32[2048,32]{0,1:T(8,128)S(1)}, u32[]{:S(2)}) copy-start(f32[2048,32]{0,1:T(8,128)S(1)} %get-tuple-element.645) | copy-start | bytes 786436
  172.0 14.9 %copy-start.4 = (bf16[3,2048,64]{2,1,0:T(8,128)(2,1)}, bf16[3,2048,64]{2,1,0:T(8,128)(2,1)S(1)}, u32[]{:S(2)}) copy-start(bf16[3,2048,64]{2,1,0:T(8,128)(2,1)S(1)} %get-tuple-element.1169) | copy-start | bytes 2359300
  172.0 14.9 %copy-start.52 = (bf16[768]{0:T(1024)(128)(2,1)S(1)}, bf16[768]{0:T(1024)(128)(2,1)}, u32[]{:S(2)}) copy-start(bf16[768]{0:T(1024)(128)(2,1)} %param.26) | copy-start | bytes 4612
  172.1 15.0 %copy-start.55 = (u32[32]{0:T(128)S(1)}, u32[32]{0:T(128)}, u32[]{:S(2)}) copy-start(u32[32]{0:T(128)} %constant.169) | copy-start | bytes 388
  172.1 67.7 %all-reduce.12.cloned.1.call-start = ((), (), s32[]{:S(2)}) async-start(), calls=%async_computation.28 | async-start | bytes 3145728
  186.9 112.7 %all-gather.23.cloned.1.call-start = ((), (), s32[]{:S(2)}) async-start(), calls=%async_computation.25 | async-start | bytes 2359296 | tf_op jit(solution)/shard_map/all_gather | solution.py:108
  187.0 277.2 %copy-start.35 = (f32[768]{0:T(1024)}, f32[768]{0:T(1024)S(1)}, u32[]{:S(2)}) copy-start(f32[768]{0:T(1024)S(1)} %convert_element_type.256) | copy-start | bytes 9220
  246.6 1.6 copy-start.6
  249.9 214.3 %copy-start.2 = (f32[512,768]{0,1:T(8,128)}, f32[512,768]{0,1:T(8,128)S(1)}, u32[]{:S(2)}) copy-start(f32[512,768]{0,1:T(8,128)S(1)} %get-tuple-element.604) | copy-start | bytes 4718596
  250.0 214.2 %copy-start.39 = (f32[512]{0:T(512)}, f32[512]{0:T(512)S(1)}, u32[]{:S(2)}) copy-start(f32[512]{0:T(512)S(1)} %get-tuple-element.646) | copy-start | bytes 6148
  250.0 214.2 %copy-start.41 = (f32[512]{0:T(512)}, f32[512]{0:T(512)S(1)}, u32[]{:S(2)}) copy-start(f32[512]{0:T(512)S(1)} %get-tuple-element.647) | copy-start | bytes 6148
  269.8 2.6 copy-start.17
  272.2 56.6 %all-gather.25.cloned.1.call-start = ((), (), s32[]{:S(2)}) async-start(), calls=%async_computation.26 | async-start | bytes 2359296 | tf_op jit(solution)/shard_map/all_gather | solution.py:108
  291.8 1.2 copy-start.28
  293.0 50.8 %reduce-scatter.19.cloned.1.call-start = ((), (), s32[]{:S(2)}) async-start(), calls=%async_computation.18 | async-start | bytes 7077888 | tf_op jit(solution)/shard_map/reduce_scatter | solution.py:116
  307.9 49.3 %reduce-scatter.21.cloned.1.call-start = ((), (), s32[]{:S(2)}) async-start(), calls=%async_computation.20 | async-start | bytes 3538944 | tf_op jit(solution)/shard_map/reduce_scatter | solution.py:141
  334.6 49.3 %all-gather.17.cloned.1.call-start = ((), (), s32[]{:S(2)}) async-start(), calls=%async_computation.21 | async-start | bytes 7077888 | tf_op jit(solution)/shard_map/all_gather | solution.py:151
  357.2 7.2 copy-start.1
  357.2 7.2 copy-start.15
  368.1 84.1 %all-reduce.14.cloned.1.call-start = ((), (), s32[]{:S(2)}) async-start(), calls=%async_computation.29 | async-start | bytes 3145728
  399.3 106.7 %all-gather.27.cloned.1.call-start = ((), (), s32[]{:S(2)}) async-start(), calls=%async_computation.27 | async-start | bytes 2359296 | tf_op jit(solution)/shard_map/all_gather | solution.py:108
  400.8 63.4 %copy-start.14 = (bf16[512,768]{0,1:T(8,128)(2,1)}, bf16[512,768]{0,1:T(8,128)(2,1)S(1)}, u32[]{:S(2)}) copy-start(bf16[512,768]{0,1:T(8,128)(2,1)S(1)} %copy.295) | copy-start | bytes 2359300
  462.6 1.6 copy-start.8
  462.9 2.0 copy-start.47
  478.6 30.1 %copy-start.31 = (bf16[384,384]{1,0:T(8,128)(2,1)S(1)}, bf16[384,384]{1,0:T(8,128)(2,1)}, u32[]{:S(2)}) copy-start(bf16[384,384]{1,0:T(8,128)(2,1)} %param.25) | copy-start | bytes 884740
  478.6 41.5 %reduce-scatter.23.cloned.1.call-start = ((), (), s32[]{:S(2)}) async-start(), calls=%async_computation.22 | async-start | bytes 2359296 | tf_op jit(solution)/shard_map/reduce_scatter | solution.py:141
  511.0 157.5 %all-gather.15.cloned.1.call-start = ((), (), s32[]{:S(2)}) async-start(), calls=%async_computation.19 | async-start | bytes 3538944 | tf_op jit(solution)/shard_map/all_gather | solution.py:123
  511.7 190.6 %all-gather.19.cloned.1.call-start = ((), (), s32[]{:S(2)}) async-start(), calls=%async_computation.23 | async-start | bytes 7077888 | tf_op jit(solution)/shard_map/all_gather | solution.py:151
  524.0 139.2 %copy-start.19 = (f32[2048,32]{0,1:T(8,128)S(1)}, f32[2048,32]{0,1:T(8,128)}, u32[]{:S(2)}) copy-start(f32[2048,32]{0,1:T(8,128)} %copy-done.18) | copy-start | bytes 786436
  668.4 1.4 copy-start.25
  672.9 6.8 copy-start.23
  673.9 20.0 %all-to-all-start.11 = ((bf16[8,576,48]{1,2,0:T(8,128)(2,1)}), bf16[8,576,48]{1,2,0:T(8,128)(2,1)S(1)}, u32[]{:S(2)}, u32[]{:S(2)}) async-start(bf16[8,576,48]{1,2,0:T(8,128)(2,1)} %bitcast.92), calls=%async_computation.15 | async-start | bytes 983040 | tf_op jit(solution)/shard_map/all_to_all | solution.py:22
  693.9 31.0 %all-to-all-start.10 = ((bf16[8,48,1152]{2,1,0:T(8,128)(2,1)}), bf16[8,48,1152]{2,1,0:T(8,128)(2,1)S(1)}, u32[]{:S(2)}, u32[]{:S(2)}) async-start(bf16[8,48,1152]{2,1,0:T(8,128)(2,1)} %pad_maximum_fusion.4), calls=%async_computation.14 | async-start | bytes 1769472 | tf_op jit(solution)/shard_map/all_to_all | solution.py:22
  697.5 105.4 %all-reduce.16.cloned.1.call-start = ((), (), s32[]{:S(2)}) async-start(), calls=%async_computation.30 | async-start | bytes 6291456
  702.3 6.7 copy-start.27
  715.4 1.4 copy-start.10
  716.8 3.3 copy-start.21
  724.9 15.1 %all-to-all-start.9 = ((bf16[8,384,48]{1,2,0:T(8,128)(2,1)}), bf16[8,384,48]{1,2,0:T(8,128)(2,1)S(1)}, u32[]{:S(2)}, u32[]{:S(2)}) async-start(bf16[8,384,48]{1,2,0:T(8,128)(2,1)} %bitcast.85), calls=%async_computation.13 | async-start | bytes 589824 | tf_op jit(solution)/shard_map/all_to_all | solution.py:22
  731.0 12.5 %copy-start.53 = (bf16[768]{0:T(1024)(128)(2,1)S(1)}, bf16[768]{0:T(1024)(128)(2,1)}, u32[]{:S(2)}) copy-start(bf16[768]{0:T(1024)(128)(2,1)} %param.21) | copy-start | bytes 4612
  739.9 25.4 %all-to-all-start.8 = ((bf16[8,48,1152]{2,1,0:T(8,128)(2,1)}), bf16[8,48,1152]{2,1,0:T(8,128)(2,1)S(1)}, u32[]{:S(2)}, u32[]{:S(2)}) async-start(bf16[8,48,1152]{2,1,0:T(8,128)(2,1)} %pad_maximum_fusion.3), calls=%async_computation.12 | async-start | bytes 1769472 | tf_op jit(solution)/shard_map/all_to_all | solution.py:22
  802.9 2.0 copy-start.30
  805.7 6.7 copy-start.7
  805.7 6.7 copy-start.38
  805.7 6.7 copy-start.44
  805.7 6.7 copy-start.46
  811.0 2.4 copy-start.51
  812.4 46.2 %copy-start.11 = (bf16[2,1,512,384]{2,3,0,1:T(8,128)(2,1)}, bf16[2,1,512,384]{2,3,0,1:T(8,128)(2,1)S(1)}, u32[]{:S(2)}) copy-start(bf16[2,1,512,384]{2,3,0,1:T(8,128)(2,1)S(1)} %copy.313) | copy-start | bytes 2359300
  859.9 3.2 copy-start.3
  859.9 3.2 copy-start.36
  859.9 3.2 copy-start.40
  859.9 3.2 copy-start.42
  859.9 3.2 copy-start.48
  859.9 3.2 copy-start.50
  867.7 3.1 copy-start.16
  (12 other events, 11.3 us)
Sparse Core Ops, SparseCore 0:
  25.0 29.8 all-gather.20
  62.1 12.6 reduce-scatter.16
  172.2 10.9 all-gather.12
  187.0 52.6 all-reduce.11
  272.4 27.2 all-gather.22
  301.6 27.2 all-gather.24
  331.1 12.6 reduce-scatter.18
  346.1 11.0 reduce-scatter.20
  368.2 15.5 all-gather.16
  399.4 52.6 all-reduce.13
  478.7 27.2 all-gather.26
  511.1 9.0 reduce-scatter.22
  521.7 12.1 all-gather.14
  668.5 15.6 all-gather.18
  715.6 87.3 all-reduce.15
where the time goes:
time: 891 us; the launch traced here: 879 us
  waiting for transfers between devices  318 us (36%)
  matrix products  161 us (18%)
  local copies, waits for them, and re-layouts  160 us (18%)
  blocking collectives  79.3 us (9%)
  other arithmetic  76.7 us (9%)
  loops' own time  47.7 us (5%)
  starting transfers between devices  20.9 us (2%)
  between operations  15.1 us (2%)
    unnamed x18, waiting for transfers between devices  141 us
    all_gather x4, waiting for transfers between devices, half_features(): joined = lax.all_gather(parts, 'col', axis=1, tiled=True)  82.2 us
    dot_general x38, matrix products, times_transposed(): lax.dot_general(left_side, right_side, (((1,), (1,)), ((), ())), preferre...  59.7 us
    dot_general x28, matrix products, matmul(): return jnp.dot(left_side, right_side, preferred_element_type=jnp.float32)  48.3 us
    unnamed x143, local copies, waits for them, and re-layouts  46.5 us
    unnamed x1, blocking collectives  39.4 us
    all_to_all x4, waiting for transfers between devices, sent_and_summed(): lax.all_to_all(pieces, axis, split_axis=0, concat_axis=0, tiled=True)  34.2 us
    dot_general x26, matrix products, transposed_times(): lax.dot_general(left_side, right_side, (((0,), (0,)), ((), ())), preferre...  30.8 us
  transfers between devices with their start and end apart: 19, of which 16 were waited for; matrix products, arithmetic and copies ran while one was open for 23% of the time, Pallas kernels for 0%

commit v1 on v0

v1 whole, which is shorter than its diff:
```python
import functools

import jax
import jax.numpy as jnp
from jax import lax
from jax.experimental import pallas as pl
from jax.experimental.pallas import tpu as pltpu
from jax.sharding import PartitionSpec as P

D = 768
HEADS = 12
HEAD_DIM = 64
LANES = 128

norm_eps = 1e-05
rope_base = 160000.0
masked_score = -1e30
VMEM_BYTES = 56 * 1024 * 1024


def matmul(left_side, right_side):
    return jnp.dot(left_side, right_side, preferred_element_type=jnp.float32)


def times_transposed(left_side, right_side):
    return lax.dot_general(
        left_side, right_side, (((1,), (1,)), ((), ())), preferred_element_type=jnp.float32
    )


def transposed_times(left_side, right_side):
    return lax.dot_general(
        left_side, right_side, (((0,), (0,)), ((), ())), preferred_element_type=jnp.float32
    )


def token_layout(lengths, slot_count):
    seq_ends = jnp.cumsum(lengths, dtype=jnp.int32)
    places = jnp.arange(slot_count, dtype=jnp.int32)
    passed = (places[:, None] >= seq_ends[None, :]).astype(jnp.int32)
    segment = jnp.sum(passed, axis=1, dtype=jnp.int32)
    position = places - jnp.sum(passed * lengths[None, :], axis=1, dtype=jnp.int32)
    return (segment, position)


def norm_forward(stream, gain_vec):
    row_mean = jnp.mean(stream, axis=1, keepdims=True)
    squares = jnp.mean(stream * stream, axis=1, keepdims=True)
    inv_std = lax.rsqrt(squares - row_mean * row_mean + norm_eps)
    normed = (stream - row_mean) * inv_std
    normed_low = (normed * gain_vec.astype(jnp.float32)).astype(jnp.bfloat16)
    return (normed, inv_std, normed_low)


def norm_backward(normed_grad, normed, inv_std, gain_vec):
    scaled = normed_grad * gain_vec.astype(jnp.float32)
    first_mean = jnp.mean(scaled, axis=1, keepdims=True)
    second_mean = jnp.mean(scaled * normed, axis=1, keepdims=True)
    stream_grad = inv_std * (scaled - first_mean - normed * second_mean)
    return (stream_grad, jnp.sum(normed_grad * normed, axis=0))


def rope_lanes(position):
    half = HEAD_DIM // 2
    lane = jnp.arange(LANES, dtype=jnp.int32)
    inv_freq = rope_base ** (-2.0 * (lane % half).astype(jnp.float32) / HEAD_DIM)
    angles = position.astype(jnp.float32)[:, None] * inv_freq[None, :]
    cos_tab, sin_tab = jnp.cos(angles), jnp.sin(angles)
    low_half = (lane < half)[None, :]
    high_half = ((lane >= half) & (lane < HEAD_DIM))[None, :]
    return (cos_tab, jnp.where(low_half, -sin_tab, 0.0), jnp.where(high_half, sin_tab, 0.0))


def mask_lanes(segment):
    lane = jnp.arange(LANES, dtype=jnp.int32)[None, :]
    used = (lane >= HEAD_DIM) & (lane < HEAD_DIM + 3)
    same = (segment[:, None] + HEAD_DIM) == lane
    query_side = jnp.where(used & ~same, masked_score, 0.0)
    key_side = jnp.where(same, 1.0, 0.0)
    ones = ((lane >= HEAD_DIM + 3) & (lane < HEAD_DIM + 6)).astype(jnp.float32)
    return (query_side.astype(jnp.bfloat16), (key_side + ones).astype(jnp.bfloat16))


def turn(u, cos_tab, low_tab, high_tab):
    half = HEAD_DIM // 2
    return (
        u * cos_tab + pltpu.roll(u, LANES - half, 1) * low_tab + pltpu.roll(u, half, 1) * high_tab
    )


def forward_kernel(
    rows, h1_ref, w_ref, cos_ref, low_ref, high_ref, fq_ref, fk_ref, qa_ref, ka_ref, va_ref, ctx_ref
):
    block = pl.program_id(1)
    total = h1_ref.shape[0]

    @pl.when(block == 0)
    def _():
        def part(i, carry):
            at = pl.ds(pl.multiple_of(i * rows, rows), rows)
            u = matmul(h1_ref[at, :], w_ref[0])
            tables = (cos_ref[at, :], low_ref[at, :], high_ref[at, :])
            lane = lax.broadcasted_iota(jnp.int32, (rows, LANES), 1)
            used = lane < HEAD_DIM
            q = turn(u[:, :LANES], *tables).astype(jnp.bfloat16).astype(jnp.float32)
            k = turn(u[:, LANES : 2 * LANES], *tables)
            v = u[:, 2 * LANES :]
            scale = HEAD_DIM**-0.5
            qa_ref[0, at, :] = jnp.where(used, q * scale, fq_ref[at, :].astype(jnp.float32)).astype(
                jnp.bfloat16
            )
            ka_ref[0, at, :] = jnp.where(used, k, fk_ref[at, :].astype(jnp.float32)).astype(
                jnp.bfloat16
            )
            ones = (lane < HEAD_DIM + 3).astype(jnp.float32)
            va_ref[0, at, :] = jnp.where(used, v, ones).astype(jnp.bfloat16)
            return carry

        lax.fori_loop(0, total // rows, part, 0)

    at = pl.ds(pl.multiple_of(block * rows, rows), rows)
    scores = times_transposed(qa_ref[0, at, :], ka_ref[0])
    peak = jnp.max(scores, axis=1, keepdims=True)
    exponent = jnp.exp(scores - peak).astype(jnp.bfloat16)
    summed = matmul(exponent, va_ref[0])
    totals = summed[:, HEAD_DIM : HEAD_DIM + 1]
    lane = lax.broadcasted_iota(jnp.int32, summed.shape, 1)
    ctx_ref[0] = jnp.where(lane < HEAD_DIM, summed / totals, peak + jnp.log(totals))


def attend_forward(h1, weights, tables, feats):
    total = h1.shape[0]
    heads = weights.shape[0]
    rows = 256
    whole = lambda shape: pl.BlockSpec(shape, lambda h, i: (0,) * len(shape))
    per_head = lambda shape: pl.BlockSpec((1, *shape), lambda h, i: (h, 0, 0))
    out = jax.ShapeDtypeStruct((heads, total, LANES), jnp.bfloat16)
    return pl.pallas_call(
        functools.partial(forward_kernel, rows),
        grid=(heads, total // rows),
        in_specs=[whole(h1.shape), per_head(weights.shape[1:])] + [whole((total, LANES))] * 5,
        out_specs=[per_head((total, LANES))] * 3
        + [pl.BlockSpec((1, rows, LANES), lambda h, i: (h, i, 0))],
        out_shape=[out, out, out, jax.ShapeDtypeStruct((heads, total, LANES), jnp.float32)],
        compiler_params=pltpu.CompilerParams(
            vmem_limit_bytes=VMEM_BYTES, dimension_semantics=("arbitrary", "arbitrary")
        ),
        cost_estimate=pl.CostEstimate(
            flops=heads * total * total * 1024, bytes_accessed=1 << 24, transcendentals=0
        ),
        name="attend_forward",
    )(h1, weights, *tables, *feats)


def backward_kernel(
    rows, qa_ref, ka_ref, va_ref, ga_ref, cos_ref, low_ref, high_ref, out_ref, dk_acc, dv_acc
):
    block = pl.program_id(1)
    last = pl.num_programs(1) - 1
    total = ka_ref.shape[1]
    at = pl.ds(pl.multiple_of(block * rows, rows), rows)
    qa = qa_ref[0, at, :]
    ga = ga_ref[0, at, :]
    probs = jnp.exp(times_transposed(ka_ref[0], qa))
    probs_low = probs.astype(jnp.bfloat16)
    dprobs = times_transposed(va_ref[0], ga)
    dscores = (probs * dprobs).astype(jnp.bfloat16)
    dv = matmul(probs_low, ga)
    dk = matmul(dscores, qa)

    @pl.when(block == 0)
    def _():
        dv_acc[...] = dv
        dk_acc[...] = dk

    @pl.when(block > 0)
    def _():
        dv_acc[...] += dv
        dk_acc[...] += dk

    dq = transposed_times(dscores, ka_ref[0]) * HEAD_DIM**-0.5
    used = lax.broadcasted_iota(jnp.int32, (rows, LANES), 1) < HEAD_DIM

    def back(u, at):
        u = jnp.where(used, u, 0.0)
        return jnp.where(used, turn(u, cos_ref[at, :], -low_ref[at, :], -high_ref[at, :]), 0.0)

    out_ref[0, at, :LANES] = back(dq, at).astype(jnp.bfloat16)

    @pl.when(block == last)
    def _():
        def part(i, carry):
            here = pl.ds(pl.multiple_of(i * rows, rows), rows)
            out_ref[0, here, LANES : 2 * LANES] = back(dk_acc[here, :], here).astype(jnp.bfloat16)
            out_ref[0, here, 2 * LANES :] = jnp.where(used, dv_acc[here, :], 0.0).astype(
                jnp.bfloat16
            )
            return carry

        lax.fori_loop(0, total // rows, part, 0)


def attend_backward(qa, ka, va, ga, tables):
    heads, total, _ = qa.shape
    rows = 256
    whole = lambda shape: pl.BlockSpec(shape, lambda h, i: (0,) * len(shape))
    per_head = lambda shape: pl.BlockSpec((1, *shape), lambda h, i: (h, 0, 0))
    return pl.pallas_call(
        functools.partial(backward_kernel, rows),
        grid=(heads, total // rows),
        in_specs=[per_head((total, LANES))] * 4 + [whole((total, LANES))] * 3,
        out_specs=per_head((total, 3 * LANES)),
        out_shape=jax.ShapeDtypeStruct((heads, total, 3 * LANES), jnp.bfloat16),
        scratch_shapes=[pltpu.VMEM((total, LANES), jnp.float32)] * 2,
        compiler_params=pltpu.CompilerParams(
            vmem_limit_bytes=VMEM_BYTES, dimension_semantics=("arbitrary", "arbitrary")
        ),
        cost_estimate=pl.CostEstimate(
            flops=heads * total * total * 2560, bytes_accessed=1 << 24, transcendentals=0
        ),
        name="attend_backward",
    )(qa, ka, va, ga, *tables)


def three_parts(values):
    high = values.astype(jnp.bfloat16)
    rest = values - high.astype(jnp.float32)
    middle = rest.astype(jnp.bfloat16)
    low = (rest - middle.astype(jnp.float32)).astype(jnp.bfloat16)
    return jnp.concatenate([high, middle, low], axis=-1)


def swap_tokens_for_heads(values):
    quarter = values.shape[0]
    cut = values.reshape(quarter, 2, 2, -1).transpose(2, 1, 0, 3).reshape(4, quarter, -1)
    return lax.all_to_all(cut, ("row", "col"), split_axis=0, concat_axis=0, tiled=True).reshape(
        4 * quarter, -1
    )


def swap_heads_for_tokens(values):
    quarter = values.shape[0] // 4
    got = lax.all_to_all(
        values.reshape(4, quarter, -1), ("row", "col"), split_axis=0, concat_axis=0, tiled=True
    )
    return got.reshape(2, 2, quarter, -1).transpose(2, 1, 0, 3).reshape(quarter, -1)


def gather_quarters(values):
    return lax.all_gather(values, ("row", "col"), axis=0, tiled=True)


def whole_weight(weight, first, second):
    weight = lax.all_gather(weight, second, axis=1, tiled=True)
    return lax.all_gather(weight, first, axis=0, tiled=True)


def sum_over_packs(array, dim):
    parts = lax.axis_size("dp")
    shape = array.shape
    cut = array.reshape(*shape[:dim], parts, shape[dim] // parts, *shape[dim + 1 :])
    cut = jnp.moveaxis(cut, dim, 0)
    arrived = lax.all_to_all(cut, "dp", split_axis=0, concat_axis=0, tiled=True)
    return arrived.astype(jnp.float32).sum(axis=0)


def shards(
    layer_input,
    attn_gain,
    query_weight,
    key_weight,
    value_weight,
    out_weight,
    mlp_gain,
    act_weight,
    lin_weight,
    down_weight,
    seq_lengths,
    output_grad,
):
    bf16 = jnp.bfloat16
    stream = layer_input.astype(jnp.float32)
    quarter = stream.shape[0]
    total = quarter * 4
    segment, position = token_layout(seq_lengths[0], total)
    tables = rope_lanes(position)
    feats = mask_lanes(segment)
    normed_attn, inv_attn, low_attn = norm_forward(stream, attn_gain)

    stacked = jnp.stack((query_weight, key_weight, value_weight), axis=1)
    own = lax.all_to_all(stacked, "row", split_axis=2, concat_axis=0, tiled=True)
    own_heads = own.shape[2] // HEAD_DIM
    per_head = own.reshape(D, 3, own_heads, HEAD_DIM).transpose(2, 0, 1, 3)
    head_weights = jnp.pad(per_head, ((0, 0), (0, 0), (0, 0), (0, LANES - HEAD_DIM))).reshape(
        own_heads, D, 3 * LANES
    )

    h1 = gather_quarters(low_attn)
    qa, ka, va, ctx = attend_forward(h1, head_weights, tables, feats)
    context_heads = ctx[:, :, :HEAD_DIM]
    context_own = context_heads.astype(bf16).transpose(1, 0, 2).reshape(total, -1)

    out_whole = whole_weight(out_weight, "col", "row")
    act_whole = whole_weight(act_weight, "row", "col")
    lin_whole = whole_weight(lin_weight, "row", "col")
    down_whole = whole_weight(down_weight, "col", "row")

    context = swap_heads_for_tokens(context_own)
    middle = stream + matmul(context, out_whole)
    normed_mlp, inv_mlp, low_mlp = norm_forward(middle, mlp_gain)
    act = matmul(low_mlp, act_whole)
    lin = matmul(low_mlp, lin_whole)
    cdf = 0.5 * (1.0 + lax.erf(act * (0.5**0.5)))
    gelu = act * cdf
    hidden = (gelu * lin).astype(bf16)
    layer_output = (middle + matmul(hidden, down_whole)).astype(bf16)

    top_grad = output_grad.astype(jnp.float32)
    grad_down = transposed_times(hidden, output_grad).astype(bf16)
    hidden_grad = times_transposed(output_grad, down_whole)
    pdf = jnp.exp(-0.5 * act * act) * (0.5 / jnp.pi) ** 0.5
    act_grad = (hidden_grad * lin * (cdf + act * pdf)).astype(bf16)
    lin_grad = (hidden_grad * gelu).astype(bf16)
    grad_act = transposed_times(low_mlp, act_grad).astype(bf16)
    grad_lin = transposed_times(low_mlp, lin_grad).astype(bf16)
    mlp_norm_grad = times_transposed(act_grad, act_whole) + times_transposed(lin_grad, lin_whole)
    middle_back, gain_mlp_part = norm_backward(mlp_norm_grad, normed_mlp, inv_mlp, mlp_gain)
    middle_grad = top_grad + middle_back
    attn_grad = middle_grad.astype(bf16)
    grad_out = transposed_times(context, attn_grad).astype(bf16)
    context_grad = times_transposed(attn_grad, out_whole).astype(bf16)
    grad_own = swap_tokens_for_heads(context_grad)

    grad_heads = grad_own.reshape(total, own_heads, HEAD_DIM).transpose(1, 0, 2)
    inner = jnp.sum(grad_heads.astype(jnp.float32) * context_heads, axis=2, keepdims=True)
    ga = jnp.pad(
        jnp.concatenate([grad_heads, three_parts(-inner)], axis=2),
        ((0, 0), (0, 0), (0, LANES - HEAD_DIM - 3)),
    )
    minus_total = three_parts(-ctx[:, :, HEAD_DIM : HEAD_DIM + 1])
    qa = jnp.concatenate(
        [qa[:, :, : HEAD_DIM + 3], minus_total, qa[:, :, HEAD_DIM + 6 :]], axis=2
    )
    qkv_grad = attend_backward(qa, ka, va, ga, tables)

    norm_partial = lax.dot_general(
        qkv_grad,
        head_weights,
        (((0, 2), (0, 2)), ((), ())),
        preferred_element_type=jnp.float32,
    ).astype(bf16)
    pieces = lax.all_to_all(
        norm_partial.reshape(4, quarter, D), ("row", "col"), split_axis=0, concat_axis=0, tiled=True
    )
    attn_norm_grad = pieces.astype(jnp.float32).sum(axis=0)
    head_grads = lax.dot_general(
        h1, qkv_grad, (((0,), (1,)), ((), ())), preferred_element_type=jnp.float32
    ).astype(bf16)
    head_grads = head_grads.reshape(D, own_heads, 3, LANES)[..., :HEAD_DIM]
    head_grads = head_grads.transpose(0, 2, 1, 3).reshape(D, 3, own_heads * HEAD_DIM)
    attn_weight_grad = lax.all_to_all(head_grads, "row", split_axis=0, concat_axis=2, tiled=True)
    stream_back, gain_attn_part = norm_backward(attn_norm_grad, normed_attn, inv_attn, attn_gain)
    grad_input = middle_grad + stream_back

    def over_group(array, first, second):
        array = lax.psum_scatter(array, first, scatter_dimension=0, tiled=True)
        return lax.psum_scatter(array, second, scatter_dimension=1, tiled=True)

    grad_out = sum_over_packs(over_group(grad_out, "col", "row"), 1)
    grad_down = sum_over_packs(over_group(grad_down, "col", "row"), 1)
    grad_act = sum_over_packs(over_group(grad_act, "row", "col"), 0)
    grad_lin = sum_over_packs(over_group(grad_lin, "row", "col"), 0)
    qkv_sums = sum_over_packs(attn_weight_grad, 0)
    gains = lax.psum_scatter(
        jnp.stack((gain_attn_part, gain_mlp_part), axis=1),
        ("dp", "row", "col"),
        scatter_dimension=0,
        tiled=True,
    )
    return (
        layer_output,
        grad_input,
        gains[:, 0],
        qkv_sums[:, 0],
        qkv_sums[:, 1],
        qkv_sums[:, 2],
        grad_out,
        gains[:, 1],
        grad_act,
        grad_lin,
        grad_down,
    )


def solution(mesh):
    in_specs = (
        P(("dp", "row", "col"), None),
        P(),
        P("row", "col"),
        P("row", "col"),
        P("row", "col"),
        P("col", "row"),
        P(),
        P("row", "col"),
        P("row", "col"),
        P("col", "row"),
        P("dp", None),
        P(("dp", "row", "col"), None),
    )
    out_specs = (
        P(("dp", "row", "col"), None),
        P(("dp", "row", "col"), None),
        P(("dp", "row", "col")),
        P(("row", "dp"), "col"),
        P(("row", "dp"), "col"),
        P(("row", "dp"), "col"),
        P("col", ("row", "dp")),
        P(("dp", "row", "col")),
        P(("row", "dp"), "col"),
        P(("row", "dp"), "col"),
        P("col", ("row", "dp")),
    )
    return jax.shard_map(shards, mesh=mesh, in_specs=in_specs, out_specs=out_specs, check_vma=False)
```

time: 891 us -> 499 us (0.56)
  waiting for transfers between devices: 318 us -> 107 us
  matrix products: 161 us -> 52.8 us
  local copies, waits for them, and re-layouts: 160 us -> 59.8 us
  Pallas kernels: 0 us -> 98 us
  loops' own time: 47.7 us -> 0 us
  other arithmetic: 76.7 us -> 35.1 us
  starting transfers between devices: 20.9 us -> 38.7 us
    unnamed x18 -> x17, waiting for transfers between devices: 141 us -> 0.26 us
    pallas_call x0 -> x2, Pallas kernels: none -> 98 us  [the longest x1 56.7 us: attend_backward(): pl.pallas_call(functools.partial(backward_kernel, rows), grid=(heads, tot...]
    all_gather x8 -> x5, waiting for transfers between devices: 109 us -> 10.8 us  [the longest x4 10.8 us: whole_weight(): return lax.all_gather(weight, first, axis=0, tiled=True)]
    dot_general x38 -> x4, matrix products: 59.7 us -> 9.88 us  [times_transposed(): lax.dot_general(left_side, right_side, (((1,), (1,)), ((), ())), preferre...]
    another operation x8 -> x0, loops' own time: 47.7 us -> none  [the longest x3 23.7 us: one_head(): lax.scan(one_block, (zeros_init, zeros_init), starts)]
    all_to_all x4 -> x9, waiting for transfers between devices: 34.2 us -> 81.8 us  [the longest x1 44 us: shards(): lax.all_to_all(norm_partial.reshape(4, quarter, D), ('row', 'col'), split...]
    all_gather x0 -> x4, blocking collectives: none -> 39.7 us  [whole_weight(): weight = lax.all_gather(weight, second, axis=1, tiled=True)]
    all_to_all x8 -> x1, blocking collectives: 39.8 us -> 5 us  [shards(): lax.all_to_all(head_grads, 'row', split_axis=0, concat_axis=2, tiled=True)]
  transfers between devices with their start and end apart: 19 -> 22, of which waited for: 16 -> 8; matrix products, arithmetic and copies ran while one was open for 23% -> 26% of each run, Pallas kernels for 0% -> 20%
where the time goes in v1:
time: 499 us; the launch traced here: 491 us
  waiting for transfers between devices  107 us (21%)
  Pallas kernels  98 us (20%)
  blocking collectives  85 us (17%)
  local copies, waits for them, and re-layouts  59.8 us (12%)
  matrix products  52.8 us (11%)
  starting transfers between devices  38.7 us (8%)
  other arithmetic  35.1 us (7%)
  between operations  14.8 us (3%)
    pallas_call x1, Pallas kernels, attend_backward(): pl.pallas_call(functools.partial(backward_kernel, rows), grid=(heads, tot...  56.7 us
    all_to_all x1, waiting for transfers between devices, shards(): lax.all_to_all(norm_partial.reshape(4, quarter, D), ('row', 'col'), split...  44 us
    pallas_call x1, Pallas kernels, attend_forward(): pl.pallas_call(functools.partial(forward_kernel, rows), grid=(heads, tota...  41.3 us
    unnamed x1, blocking collectives  40.2 us
    all_gather x4, blocking collectives, whole_weight(): weight = lax.all_gather(weight, second, axis=1, tiled=True)  39.7 us
    all_to_all x5, waiting for transfers between devices, sum_over_packs(): arrived = lax.all_to_all(cut, 'dp', split_axis=0, concat_axis=0, tiled=True)  29.2 us
    all_to_all x5, starting transfers between devices, sum_over_packs(): arrived = lax.all_to_all(cut, 'dp', split_axis=0, concat_axis=0, tiled=True)  22.5 us
    unnamed x83, local copies, waits for them, and re-layouts  17.2 us
  transfers between devices with their start and end apart: 22, of which 8 were waited for; matrix products, arithmetic and copies ran while one was open for 26% of the time, Pallas kernels for 20%

profile of v1, /device:TPU:0, one launch (start us, length us, event | category | flops | bytes accessed | tf_op | source)
XLA Modules:
  0.0 491.3 jit_solution(16210552306489737952)
XLA Ops:
  9.4 2.4 fusion.22
  11.9 2.4 all_gather.28
  14.4 19.3 %all_gather.30 = bf16[384,1152]{0,1:T(8,128)(2,1)} all-gather(bf16[384,576]{0,1:T(8,128)(2,1)S(1)} %copy-done.23), channel_id=1, replica_groups=mesh['dp'=8,'row'=2,'col'=2] {'col'}, dimensions={1}, use_global_device_ids=true | all-gather | bytes 1327104 | tf_op jit(solution)/shard_map/all_gather | solution.py:254
  33.9 2.0 copy.111
  36.0 3.7 all-to-all-start
  39.8 15.2 %all_gather.32 = bf16[384,1152]{0,1:T(8,128)(2,1)} all-gather(bf16[384,576]{0,1:T(8,128)(2,1)S(1)} %copy-done.24), channel_id=1, replica_groups=mesh['dp'=8,'row'=2,'col'=2] {'col'}, dimensions={1}, use_global_device_ids=true | all-gather | bytes 1327104 | tf_op jit(solution)/shard_map/all_gather | solution.py:254
  57.0 2.5 copy.115.w_ref
  61.1 5.9 %fusion.33 = (f32[2048,128]{1,0:T(8,128)}, f32[2048,128]{1,0:T(8,128)}, f32[2048,128]{1,0:T(8,128)}) fusion(f32[128]{0:T(128)S(1)} %fusion.42, f32[2048]{0:T(1024)S(1)} %get-tuple-element.57, pred[128]{0:T(512)(128)(4,1)S(1)} %get-tuple-element.59, pred[128]{0:T(512)(128)(4,1)S(1)} %get-tuple-element.60), kind=kLoop, calls=%fused_computation.62 | loop fusion | flops 1048576 | bytes 3154688 | tf_op jit(solution)/shard_map/jit(_where)/select_n | solution.py:71
  66.9 41.3 %attend_forward.1 = (bf16[3,2048,128]{2,1,0:T(8,128)(2,1)}, bf16[3,2048,128]{2,1,0:T(8,128)(2,1)}, bf16[3,2048,128]{2,1,0:T(8,128)(2,1)}, f32[3,2048,128]{2,1,0:T(8,128)}) custom-call(bf16[2048,768]{1,0:T(8,128)(2,1)} %all-gather.6.cloned.1.call-done.h1_ref, bf16[3,768,384]{2,1,0:T(8,128)(2,1)} %copy.115.w_ref, f32[2048,128]{1,0:T(8,128)} %get-tuple-element.46.cos_ref, ...), custom_call_target="tpu_custom_call" | custom-call | flops 12884901888 | bytes 16777216 | tf_op jit(solution)/shard_map/attend_forward/pallas_call | solution.py:138
  108.2 2.1 fusion.29
  112.6 3.6 all-to-all-start.1
  116.3 2.7 all_gather.34
  119.3 8.5 %all-to-all-done.1 = bf16[4,512,192]{1,2,0:T(8,128)(2,1)S(1)} async-done(((bf16[4,512,192]{1,2,0:T(8,128)(2,1)}), bf16[4,512,192]{1,2,0:T(8,128)(2,1)S(1)}, u32[]{:S(2)}, u32[]{:S(2)}) %all-to-all-start.1) | async-done | bytes 786464 | tf_op jit(solution)/shard_map/all_to_all | solution.py:243
  127.9 2.6 fusion.44
  130.9 4.7 fusion.47
  135.6 4.2 fusion.48
  139.8 10.7 %all-gather.14.cloned.1.call-done = bf16[1152,768]{1,0:T(8,128)(2,1)} async-done(((bf16[576,768]{1,0:T(8,128)(2,1)}), bf16[1152,768]{1,0:T(8,128)(2,1)}) %all-gather.14.cloned.1.call-update) | async-done | bytes 1769488 | tf_op jit(solution)/shard_map/all_gather | solution.py:255
  150.5 5.0 %multiply_convert_fusion = (bf16[512,1152]{1,0:T(8,128)(2,1)S(1)}, bf16[512,1152]{1,0:T(8,128)(2,1)S(1)}, bf16[512,1152]{1,0:T(8,128)(2,1)}) fusion(f32[512,1152]{1,0:T(8,128)} %fusion.47, f32[512,1152]{1,0:T(8,128)} %fusion.48, bf16[512,768]{1,0:T(8,128)(2,1)S(1)} %copy-done.19, bf16[1152,768]{1,0:T(8,128)(2,1)} %all-gather.14.cloned.1.call-done), kind=kOutput, calls=%fused_computation.30 | convolution fusion | flops 915406848 | bytes 10813440 | tf_op jit(solution)/shard_map/dot_general | solution.py:26
  160.6 1.8 convolution_convert_fusion.3
  162.5 3.7 convolution_convert_fusion.2
  166.3 3.7 convolution_convert_fusion.1
  170.1 14.3 %reduce-scatter.18.cloned.1.call-done = bf16[384,768]{1,0:T(8,128)(2,1)} async-done(((bf16[768,768]{1,0:T(8,128)(2,1)}), bf16[384,768]{1,0:T(8,128)(2,1)}) %reduce-scatter.18.cloned.1.call-update) | async-done | bytes 589840 | tf_op jit(solution)/shard_map/reduce_scatter | solution.py:366
  184.3 2.1 copy.138
  186.5 2.1 convolution_convert_fusion.4
  189.8 2.3 copy.120
  192.0 4.2 all-to-all-start.2
  196.5 3.1 subtract_convert_fusion.1
  199.6 1.6 slice.33
  201.2 9.2 %concatenate.6.qa_ref = bf16[3,2048,128]{2,1,0:T(8,128)(2,1)} concatenate(bf16[3,2048,67]{2,1,0:T(8,128)(2,1)} %bitcast.110, bf16[3,2048,1]{2,1,0:T(8,128)(2,1)} %get-tuple-element.33, bf16[3,2048,1]{2,1,0:T(8,128)(2,1)} %get-tuple-element.32, bf16[3,2048,1]{2,1,0:T(8,128)(2,1)} %get-tuple-element.31, bf16[3,2048,58]{2,1,0:T(8,128)(2,1)} %slice.33), dimensions={2} | concatenate | bytes 3145728 | tf_op jit(solution)/shard_map/concatenate | solution.py:341
  210.4 3.9 convolution_convert_fusion
  214.3 2.6 copy.121
  217.0 2.8 reshape_reshape.7
  219.8 2.5 copy.122
  222.2 2.3 multiply_reduce_fusion
  225.3 1.6 copy.125
  226.9 2.2 copy.123
  229.1 2.8 subtract_convert_fusion.2
  232.3 3.5 fusion.32.ga_ref
  235.8 56.7 %attend_backward.1 = bf16[3,2048,384]{2,1,0:T(8,128)(2,1)} custom-call(bf16[3,2048,128]{2,1,0:T(8,128)(2,1)} %concatenate.6.qa_ref, bf16[3,2048,128]{2,1,0:T(8,128)(2,1)} %get-tuple-element.17.ka_ref, bf16[3,2048,128]{2,1,0:T(8,128)(2,1)} %get-tuple-element.18.va_ref, bf16[3,2048,128]{2,1,0:T(8,128)(2,1)} %fusion.32.ga_ref, ...), custom_call_target="tpu_custom_call" | custom-call | flops 32212254720 | bytes 16777216 | tf_op jit(solution)/shard_map/attend_backward/pallas_call | solution.py:208
  292.6 6.2 %fusion.14 = bf16[768,3,384]{0,2,1:T(8,128)(2,1)S(1)} fusion(bf16[3,2048,384]{2,1,0:T(8,128)(2,1)} %attend_backward.1, bf16[2048,768]{1,0:T(8,128)(2,1)S(1)} %copy-done.32), kind=kOutput, calls=%fused_computation.35 | convolution fusion | flops 3624763392 | bytes 9633792 | tf_op jit(solution)/shard_map/dot_general | solution.py:356
  299.9 5.0 %all_to_all.70 = bf16[768,3,192]{2,1,0:T(4,128)(2,1)S(1)} all-to-all(bf16[768,3,192]{2,1,0:T(4,128)(2,1)S(1)} %copy.129), channel_id=1, replica_groups=mesh['dp'=8,'row'=2,'col'=2] {'row'}, dimensions={0} | all-to-all | bytes 1769472 | tf_op jit(solution)/shard_map/all_to_all | solution.py:361
  307.9 5.7 %all-to-all-start.5 = ((bf16[8,48,3,384]{3,1,2,0:T(8,128)(2,1)}), bf16[8,48,3,384]{3,1,2,0:T(8,128)(2,1)S(1)}, u32[]{:S(2)}, u32[]{:S(2)}) async-start(bf16[8,48,3,384]{3,1,2,0:T(8,128)(2,1)} %copy.131), calls=%async_computation.5 | async-start | bytes 1769472 | tf_op jit(solution)/shard_map/all_to_all | solution.py:263
  313.7 2.3 copy.140
  316.1 8.0 %bitcast_convert_fusion = bf16[2048,768]{1,0:T(8,128)(2,1)} fusion(bf16[3,2048,384]{2,1,0:T(8,128)(2,1)} %attend_backward.1, bf16[3,768,384]{1,2,0:T(8,128)(2,1)S(1)} %bitcast.109), kind=kOutput, calls=%fused_computation | convolution fusion | flops 3625451520 | bytes 9633792 | tf_op jit(solution)/shard_map/dot_general | solution.py:346
  324.1 12.1 %all-to-all-done.5 = bf16[8,48,3,384]{3,1,2,0:T(8,128)(2,1)S(1)} async-done(((bf16[8,48,3,384]{3,1,2,0:T(8,128)(2,1)}), bf16[8,48,3,384]{3,1,2,0:T(8,128)(2,1)S(1)}, u32[]{:S(2)}, u32[]{:S(2)}) %all-to-all-start.5) | async-done | bytes 884768 | tf_op jit(solution)/shard_map/all_to_all | solution.py:263
  337.2 3.7 all-to-all-start.3
  341.0 2.2 copy.142
  343.2 44.0 %all-to-all-done.3 = bf16[4,512,768]{2,1,0:T(8,128)(2,1)S(1)} async-done(((bf16[4,512,768]{2,1,0:T(8,128)(2,1)}), bf16[4,512,768]{2,1,0:T(8,128)(2,1)S(1)}, u32[]{:S(2)}, u32[]{:S(2)}) %all-to-all-start.3) | async-done | bytes 3145760 | tf_op jit(solution)/shard_map/all_to_all | solution.py:352
  387.3 3.6 all-to-all-start.6
  391.0 2.2 copy.144
  393.3 2.1 copy.141
  395.4 4.9 all-to-all-done.6
  400.3 3.6 all-to-all-start.7
  403.9 4.0 add_convert_fusion
  409.3 2.0 copy.143
  411.3 6.1 %all-to-all-done.7 = bf16[8,48,576]{2,1,0:T(8,128)(2,1)S(1)} async-done(((bf16[8,48,576]{2,1,0:T(8,128)(2,1)}), bf16[8,48,576]{2,1,0:T(8,128)(2,1)S(1)}, u32[]{:S(2)}, u32[]{:S(2)}) %all-to-all-start.7) | async-done | bytes 442400 | tf_op jit(solution)/shard_map/all_to_all | solution.py:263
  418.2 4.3 all-to-all-start.8
  422.5 2.0 fusion.27
  424.5 40.2 %all-reduce.2 = f32[768,2]{0,1:T(2,128)S(1)} all-reduce(f32[768,2]{0,1:T(2,128)S(1)} %pad_maximum_fusion.1), channel_id=2, replica_groups=mesh['dp'=8,'row'=2,'col'=2] {'dp','row','col'}, use_global_device_ids=true, to_apply=%region_15.16.clone | all-reduce | flops 1536 | bytes 12288
  464.8 5.3 %all-to-all-start.9 = ((bf16[8,576,48]{1,2,0:T(8,128)(2,1)}), bf16[8,576,48]{1,2,0:T(8,128)(2,1)}, u32[]{:S(2)}, u32[]{:S(2)}) async-start(bf16[8,576,48]{1,2,0:T(8,128)(2,1)} %bitcast.126), calls=%async_computation.13 | async-start | bytes 983040 | tf_op jit(solution)/shard_map/all_to_all | solution.py:263
  470.6 2.9 fusion.26
  474.9 1.8 convert_reduce_fusion.4
  476.6 6.2 %all-to-all-done.9 = bf16[8,576,48]{1,2,0:T(8,128)(2,1)} async-done(((bf16[8,576,48]{1,2,0:T(8,128)(2,1)}), bf16[8,576,48]{1,2,0:T(8,128)(2,1)}, u32[]{:S(2)}, u32[]{:S(2)}) %all-to-all-start.9) | async-done | bytes 442400 | tf_op jit(solution)/shard_map/all_to_all | solution.py:263
  482.8 1.8 convert_reduce_fusion.3
  (163 shorter events, 26.2 us)
Async XLA Ops:
  7.2 59.8 %all-gather.6.cloned.1.call-start = ((), (), s32[]{:S(2)}) async-start(), calls=%async_computation.18 | async-start | bytes 3932160 | tf_op jit(solution)/shard_map/all_gather | solution.py:250
  7.9 4.0 copy-start.26
  9.4 5.0 %copy-start.23 = (bf16[384,576]{0,1:T(8,128)(2,1)S(1)}, bf16[384,576]{0,1:T(8,128)(2,1)}, u32[]{:S(2)}) copy-start(bf16[384,576]{0,1:T(8,128)(2,1)} %param.19) | copy-start | bytes 1327108
  11.8 116.1 %all-gather.8.cloned.1.call-start = ((), (), s32[]{:S(2)}) async-start(), calls=%async_computation.19 | async-start | bytes 1769472 | tf_op jit(solution)/shard_map/all_gather | solution.py:255
  14.3 19.4 %copy-start.27 = (bf16[384,384]{1,0:T(8,128)(2,1)S(1)}, bf16[384,384]{1,0:T(8,128)(2,1)}, u32[]{:S(2)}) copy-start(bf16[384,384]{1,0:T(8,128)(2,1)} %param.16) | copy-start | bytes 884740
  14.3 19.4 %copy-start.28 = (bf16[384,384]{1,0:T(8,128)(2,1)S(1)}, bf16[384,384]{1,0:T(8,128)(2,1)}, u32[]{:S(2)}) copy-start(bf16[384,384]{1,0:T(8,128)(2,1)} %param.15) | copy-start | bytes 884740
  14.3 19.5 %copy-start.29 = (bf16[384,384]{1,0:T(8,128)(2,1)S(1)}, bf16[384,384]{1,0:T(8,128)(2,1)}, u32[]{:S(2)}) copy-start(bf16[384,384]{1,0:T(8,128)(2,1)} %param.14) | copy-start | bytes 884740
  14.4 116.5 %all-gather.10.cloned.1.call-start = ((), (), s32[]{:S(2)}) async-start(), calls=%async_computation.20 | async-start | bytes 2654208 | tf_op jit(solution)/shard_map/all_gather | solution.py:255
  36.0 3.8 copy-start.24
  36.0 19.1 %all-to-all-start = ((bf16[384,3,384]{0,1,2:T(4,128)(2,1)}), bf16[384,3,384]{0,1,2:T(4,128)(2,1)S(1)}, u32[]{:S(2)}, u32[]{:S(2)}) async-start(bf16[384,3,384]{0,1,2:T(4,128)(2,1)} %copy.111), calls=%async_computation | async-start | bytes 2359296 | tf_op jit(solution)/shard_map/all_to_all | solution.py:291
  39.7 95.9 %all-gather.12.cloned.1.call-start = ((), (), s32[]{:S(2)}) async-start(), calls=%async_computation.21 | async-start | bytes 2654208 | tf_op jit(solution)/shard_map/all_gather | solution.py:255
  56.9 2.5 copy-start.7
  56.9 2.5 copy-start.31
  111.5 4.7 copy-start.25
  112.6 6.7 %copy-start.30 = (bf16[768]{0:T(1024)(128)(2,1)S(1)}, bf16[768]{0:T(1024)(128)(2,1)}, u32[]{:S(2)}) copy-start(bf16[768]{0:T(1024)(128)(2,1)} %param.18) | copy-start | bytes 4612
  112.6 15.3 %all-to-all-start.1 = ((bf16[4,512,192]{1,2,0:T(8,128)(2,1)}), bf16[4,512,192]{1,2,0:T(8,128)(2,1)S(1)}, u32[]{:S(2)}, u32[]{:S(2)}) async-start(bf16[4,512,192]{1,2,0:T(8,128)(2,1)} %copy.117), calls=%async_computation.1 | async-start | bytes 1572864 | tf_op jit(solution)/shard_map/all_to_all | solution.py:243
  116.2 11.7 %copy-start.6 = (bf16[512,768]{1,0:T(8,128)(2,1)S(1)}, bf16[512,768]{1,0:T(8,128)(2,1)}, u32[]{:S(2)}) copy-start(bf16[512,768]{1,0:T(8,128)(2,1)} %param.12) | copy-start | bytes 2359300
  116.2 34.3 %all-gather.14.cloned.1.call-start = ((), (), s32[]{:S(2)}) async-start(), calls=%async_computation.22 | async-start | bytes 2654208 | tf_op jit(solution)/shard_map/all_gather | solution.py:255
  119.0 65.3 %reduce-scatter.18.cloned.1.call-start = ((), (), s32[]{:S(2)}) async-start(), calls=%async_computation.23 | async-start | bytes 1769472 | tf_op jit(solution)/shard_map/reduce_scatter | solution.py:366
  127.9 2.6 copy-start.15
  130.5 29.0 %copy-start.10 = (f32[512,768]{1,0:T(8,128)}, f32[512,768]{1,0:T(8,128)S(1)}, u32[]{:S(2)}) copy-start(f32[512,768]{1,0:T(8,128)S(1)} %get-tuple-element.55) | copy-start | bytes 4718596
  130.8 4.8 copy-start.21
  135.6 14.9 %copy-start.19 = (bf16[512,768]{1,0:T(8,128)(2,1)S(1)}, bf16[512,768]{1,0:T(8,128)(2,1)}, u32[]{:S(2)}) copy-start(bf16[512,768]{1,0:T(8,128)(2,1)} %param.23) | copy-start | bytes 2359300
  150.5 5.0 %copy-start.33 = (bf16[768,1152]{0,1:T(8,128)(2,1)S(1)}, bf16[768,1152]{0,1:T(8,128)(2,1)}, u32[]{:S(2)}) copy-start(bf16[768,1152]{0,1:T(8,128)(2,1)} %all-gather.10.cloned.1.call-done) | copy-start | bytes 5308420
  155.5 1.2 copy-start.36
  155.5 1.4 copy-start.35
  155.5 2.3 copy-start.34
  157.9 1.6 copy-start.20
  159.5 1.1 copy-start.16
  160.6 25.9 %copy-start.1 = (f32[512,768]{1,0:T(8,128)}, f32[512,768]{1,0:T(8,128)S(1)}, u32[]{:S(2)}) copy-start(f32[512,768]{1,0:T(8,128)S(1)} %multiply_add_fusion) | copy-start | bytes 4718596
  160.6 1.9 copy-start.22
  162.4 151.3 %reduce-scatter.20.cloned.1.call-start = ((), (), s32[]{:S(2)}) async-start(), calls=%async_computation.24 | async-start | bytes 2654208 | tf_op jit(solution)/shard_map/reduce_scatter | solution.py:366
  166.2 174.7 %reduce-scatter.22.cloned.1.call-start = ((), (), s32[]{:S(2)}) async-start(), calls=%async_computation.25 | async-start | bytes 2654208 | tf_op jit(solution)/shard_map/reduce_scatter | solution.py:366
  170.0 217.2 %reduce-scatter.26.cloned.1.call-start = ((), (), s32[]{:S(2)}) async-start(), calls=%async_computation.27 | async-start | bytes 884736
  189.8 6.7 %copy-start = (f32[3,2048,128]{2,1,0:T(8,128)S(1)}, f32[3,2048,128]{2,1,0:T(8,128)}, u32[]{:S(2)}) copy-start(f32[3,2048,128]{2,1,0:T(8,128)} %get-tuple-element.15) | copy-start | bytes 9437188
  192.0 22.3 %all-to-all-start.2 = ((bf16[4,512,192]{1,2,0:T(8,128)(2,1)}), bf16[4,512,192]{1,2,0:T(8,128)(2,1)}, u32[]{:S(2)}, u32[]{:S(2)}) async-start(bf16[4,512,192]{1,2,0:T(8,128)(2,1)} %bitcast.122), calls=%async_computation.2 | async-start | bytes 1572864 | tf_op jit(solution)/shard_map/all_to_all | solution.py:236
  196.2 194.8 %reduce-scatter.24.cloned.1.call-start = ((), (), s32[]{:S(2)}) async-start(), calls=%async_computation.26 | async-start | bytes 2654208 | tf_op jit(solution)/shard_map/reduce_scatter | solution.py:366
  196.5 3.1 copy-start.9
  229.1 2.8 copy-start.3
  229.1 3.2 copy-start.12
  235.8 56.7 %copy-start.32 = (bf16[2048,768]{1,0:T(8,128)(2,1)S(1)}, bf16[2048,768]{1,0:T(8,128)(2,1)}, u32[]{:S(2)}) copy-start(bf16[2048,768]{1,0:T(8,128)(2,1)} %all-gather.6.cloned.1.call-done.h1_ref) | copy-start | bytes 9437188
  307.9 28.3 %all-to-all-start.5 = ((bf16[8,48,3,384]{3,1,2,0:T(8,128)(2,1)}), bf16[8,48,3,384]{3,1,2,0:T(8,128)(2,1)S(1)}, u32[]{:S(2)}, u32[]{:S(2)}) async-start(bf16[8,48,3,384]{3,1,2,0:T(8,128)(2,1)} %copy.131), calls=%async_computation.5 | async-start | bytes 1769472 | tf_op jit(solution)/shard_map/all_to_all | solution.py:263
  313.6 2.4 copy-start.8
  313.6 79.6 %reduce-scatter.28.cloned.1.call-start = ((), (), s32[]{:S(2)}) async-start(), calls=%async_computation.28 | async-start | bytes 1327104
  336.2 1.0 copy-start.13
  337.2 50.1 %all-to-all-start.3 = ((bf16[4,512,768]{2,1,0:T(8,128)(2,1)}), bf16[4,512,768]{2,1,0:T(8,128)(2,1)S(1)}, u32[]{:S(2)}, u32[]{:S(2)}) async-start(bf16[4,512,768]{2,1,0:T(8,128)(2,1)} %bitcast.121), calls=%async_computation.3 | async-start | bytes 6291456 | tf_op jit(solution)/shard_map/all_to_all | solution.py:352
  340.9 68.4 %reduce-scatter.30.cloned.1.call-start = ((), (), s32[]{:S(2)}) async-start(), calls=%async_computation.29 | async-start | bytes 1327104
  387.3 6.0 %copy-start.4 = (bf16[4,512,768]{2,1,0:T(8,128)(2,1)}, bf16[4,512,768]{2,1,0:T(8,128)(2,1)S(1)}, u32[]{:S(2)}) copy-start(bf16[4,512,768]{2,1,0:T(8,128)(2,1)S(1)} %all-to-all-done.3) | copy-start | bytes 9437188
  387.3 13.1 %all-to-all-start.6 = ((bf16[8,384,48]{1,2,0:T(8,128)(2,1)}), bf16[8,384,48]{1,2,0:T(8,128)(2,1)S(1)}, u32[]{:S(2)}, u32[]{:S(2)}) async-start(bf16[8,384,48]{1,2,0:T(8,128)(2,1)} %bitcast.133), calls=%async_computation.7 | async-start | bytes 589824 | tf_op jit(solution)/shard_map/all_to_all | solution.py:263
  390.9 73.9 %reduce-scatter.32.cloned.1.call-start = ((), (), s32[]{:S(2)}) async-start(), calls=%async_computation.30 | async-start | bytes 1474560
  393.3 10.7 %copy-start.11 = (f32[512,768]{1,0:T(8,128)S(1)}, f32[512,768]{1,0:T(8,128)}, u32[]{:S(2)}) copy-start(f32[512,768]{1,0:T(8,128)} %copy-done.10) | copy-start | bytes 4718596
  400.3 17.0 %all-to-all-start.7 = ((bf16[8,48,576]{2,1,0:T(8,128)(2,1)}), bf16[8,48,576]{2,1,0:T(8,128)(2,1)S(1)}, u32[]{:S(2)}, u32[]{:S(2)}) async-start(bf16[8,48,576]{2,1,0:T(8,128)(2,1)} %bitcast.34), calls=%async_computation.9 | async-start | bytes 983040 | tf_op jit(solution)/shard_map/all_to_all | solution.py:263
  403.9 4.1 copy-start.14
  403.9 4.9 copy-start.5
  417.4 0.8 copy-start.17
  418.2 46.6 %all-to-all-start.8 = ((bf16[8,48,576]{2,1,0:T(8,128)(2,1)}), bf16[8,48,576]{2,1,0:T(8,128)(2,1)}, u32[]{:S(2)}, u32[]{:S(2)}) async-start(bf16[8,48,576]{2,1,0:T(8,128)(2,1)} %bitcast.35), calls=%async_computation.11 | async-start | bytes 983040 | tf_op jit(solution)/shard_map/all_to_all | solution.py:263
  422.5 48.1 %copy-start.2 = (f32[512,768]{1,0:T(8,128)S(1)}, f32[512,768]{1,0:T(8,128)}, u32[]{:S(2)}) copy-start(f32[512,768]{1,0:T(8,128)} %copy-done.1) | copy-start | bytes 4718596
  464.8 18.0 %all-to-all-start.9 = ((bf16[8,576,48]{1,2,0:T(8,128)(2,1)}), bf16[8,576,48]{1,2,0:T(8,128)(2,1)}, u32[]{:S(2)}, u32[]{:S(2)}) async-start(bf16[8,576,48]{1,2,0:T(8,128)(2,1)} %bitcast.126), calls=%async_computation.13 | async-start | bytes 983040 | tf_op jit(solution)/shard_map/all_to_all | solution.py:263
  470.6 3.5 copy-start.18
Sparse Core Ops, SparseCore 0:
  12.0 36.0 all-gather.5
  49.6 24.1 all-gather.7
  75.3 10.0 all-gather.9
  86.8 11.2 all-gather.11
  119.2 31.2 all-gather.13
  162.6 21.7 reduce-scatter.17
  186.7 9.2 reduce-scatter.19
  198.3 10.4 reduce-scatter.21
  211.1 9.1 reduce-scatter.25
  222.5 29.3 reduce-scatter.23
  316.8 20.0 reduce-scatter.27
  343.8 27.6 reduce-scatter.29
  394.7 8.9 reduce-scatter.31

commit v2 on v1

--- a/solution.py
+++ b/solution.py
@@ -153,14 +153,55 @@
 
 
 def backward_kernel(
-    rows, qa_ref, ka_ref, va_ref, ga_ref, cos_ref, low_ref, high_ref, out_ref, dk_acc, dv_acc
+    rows,
+    qa_ref,
+    ka_ref,
+    va_ref,
+    g_ref,
+    ctx_ref,
+    cos_ref,
+    low_ref,
+    high_ref,
+    out_ref,
+    qa_full,
+    ga_full,
+    dk_acc,
+    dv_acc,
 ):
     block = pl.program_id(1)
     last = pl.num_programs(1) - 1
     total = ka_ref.shape[1]
+    lane = lax.broadcasted_iota(jnp.int32, (rows, LANES), 1)
+    used = lane < HEAD_DIM
+
+    def with_parts(base, first, column):
+        high = column.astype(jnp.bfloat16).astype(jnp.float32)
+        middle = (column - high).astype(jnp.bfloat16).astype(jnp.float32)
+        base = jnp.where(lane == first, high, base)
+        base = jnp.where(lane == first + 1, middle, base)
+        return jnp.where(lane == first + 2, column - high - middle, base).astype(jnp.bfloat16)
+
+    @pl.when(block == 0)
+    def _():
+        def part(i, carry):
+            here = pl.ds(pl.multiple_of(i * rows, rows), rows)
+            g = g_ref[0, here, :].astype(jnp.float32)
+            g = jnp.concatenate([g, jnp.zeros_like(g)], axis=1)
+            ctx = ctx_ref[0, here, :]
+            inner = jnp.sum(jnp.where(used, g * ctx, 0.0), axis=1, keepdims=True)
+            ga_full[here, :] = with_parts(g, HEAD_DIM, -inner)
+            qa_full[here, :] = with_parts(
+                qa_ref[0, here, :].astype(jnp.float32),
+                HEAD_DIM + 3,
+                -ctx[:, HEAD_DIM : HEAD_DIM + 1],
+            )
+            return carry
+
+        lax.fori_loop(0, total // rows, part, 0)
+
     at = pl.ds(pl.multiple_of(block * rows, rows), rows)
-    qa = qa_ref[0, at, :]
-    ga = ga_ref[0, at, :]
+    qa = qa_full[at, :]
+    ga = ga_full[at, :]
     probs = jnp.exp(times_transposed(ka_ref[0], qa))
     probs_low = probs.astype(jnp.bfloat16)
     dprobs = times_transposed(va_ref[0], ga)
@@ -179,7 +220,6 @@
         dk_acc[...] += dk
 
     dq = transposed_times(dscores, ka_ref[0]) * HEAD_DIM**-0.5
-    used = lax.broadcasted_iota(jnp.int32, (rows, LANES), 1) < HEAD_DIM
 
     def back(u, at):
         u = jnp.where(used, u, 0.0)
@@ -200,7 +240,7 @@
         lax.fori_loop(0, total // rows, part, 0)
 
 
-def attend_backward(qa, ka, va, ga, tables):
+def attend_backward(qa, ka, va, grads, ctx, tables):
     heads, total, _ = qa.shape
     rows = 256
     whole = lambda shape: pl.BlockSpec(shape, lambda h, i: (0,) * len(shape))
@@ -208,10 +248,13 @@
     return pl.pallas_call(
         functools.partial(backward_kernel, rows),
         grid=(heads, total // rows),
-        in_specs=[per_head((total, LANES))] * 4 + [whole((total, LANES))] * 3,
+        in_specs=[per_head((total, LANES))] * 3
+        + [per_head((total, HEAD_DIM)), per_head((total, LANES))]
+        + [whole((total, LANES))] * 3,
         out_specs=per_head((total, 3 * LANES)),
         out_shape=jax.ShapeDtypeStruct((heads, total, 3 * LANES), jnp.bfloat16),
-        scratch_shapes=[pltpu.VMEM((total, LANES), jnp.float32)] * 2,
+        scratch_shapes=[pltpu.VMEM((total, LANES), jnp.bfloat16)] * 2
+        + [pltpu.VMEM((total, LANES), jnp.float32)] * 2,
         compiler_params=pltpu.CompilerParams(
             vmem_limit_bytes=VMEM_BYTES, dimension_semantics=("arbitrary", "arbitrary")
         ),
@@ -219,15 +262,71 @@
             flops=heads * total * total * 2560, bytes_accessed=1 << 24, transcendentals=0
         ),
         name="attend_backward",
-    )(qa, ka, va, ga, *tables)
-
-
-def three_parts(values):
-    high = values.astype(jnp.bfloat16)
-    rest = values - high.astype(jnp.float32)
-    middle = rest.astype(jnp.bfloat16)
-    low = (rest - middle.astype(jnp.float32)).astype(jnp.bfloat16)
-    return jnp.concatenate([high, middle, low], axis=-1)
+    )(qa, ka, va, grads, ctx, *tables)
+
+
+def pack_sum_kernel(peers, x_ref, out_ref, got, send_sems, recv_sems):
+    me = lax.axis_index("dp")
+    barrier = pltpu.get_barrier_semaphore()
+    for d in range(1, peers):
+        pl.semaphore_signal(
+            barrier,
+            inc=1,
+            device_id={"dp": lax.rem(me + d, peers)},
+            device_id_type=pl.DeviceIdType.MESH,
+        )
+    pl.semaphore_wait(barrier, peers - 1)
+    copies = []
+    for d in range(1, peers):
+        peer = lax.rem(me + d, peers)
+        copy = pltpu.make_async_remote_copy(
+            src_ref=x_ref.at[peer],
+            dst_ref=got.at[d - 1],
+            send_sem=send_sems.at[d - 1],
+            recv_sem=recv_sems.at[d - 1],
+            device_id={"dp": peer},
+            device_id_type=pl.DeviceIdType.MESH,
+        )
+        copy.start()
+        copies.append(copy)
+    out_ref[...] = x_ref[me].astype(jnp.float32)
+    for d, copy in enumerate(copies):
+        copy.wait_recv()
+        out_ref[...] += got[d].astype(jnp.float32)
+    for copy in copies:
+        copy.wait_send()
+
+
+def sum_over_packs(array, collective_id):
+    peers = array.shape[0]
+    vmem = pl.BlockSpec(memory_space=pltpu.VMEM)
+    return pl.pallas_call(
+        functools.partial(pack_sum_kernel, peers),
+        in_specs=[vmem],
+        out_specs=vmem,
+        out_shape=jax.ShapeDtypeStruct(array.shape[1:], jnp.float32),
+        scratch_shapes=[
+            pltpu.VMEM((peers - 1, *array.shape[1:]), jnp.bfloat16),
+            pltpu.SemaphoreType.DMA((peers - 1,)),
+            pltpu.SemaphoreType.DMA((peers - 1,)),
+        ],
+        compiler_params=pltpu.CompilerParams(
+            vmem_limit_bytes=VMEM_BYTES, collective_id=collective_id, has_side_effects=True
+        ),
+        name="sum_over_packs",
+    )(array)
+
+
+def swapped(array, axis):
+    return lax.ppermute(array, axis, [(0, 1), (1, 0)])
+
+
+def kept_and_sent(halves, axis):
+    me = lax.axis_index(axis)
+    sent = lax.dynamic_index_in_dim(halves, 1 - me, 0, keepdims=False)
+    kept = lax.dynamic_index_in_dim(halves, me, 0, keepdims=False)
+    other = swapped(sent, axis)
+    return (kept.astype(jnp.float32) + other.astype(jnp.float32)).astype(jnp.bfloat16)
 
 
 def swap_tokens_for_heads(values):
@@ -253,15 +352,6 @@
 def whole_weight(weight, first, second):
     weight = lax.all_gather(weight, second, axis=1, tiled=True)
     return lax.all_gather(weight, first, axis=0, tiled=True)
-
-
-def sum_over_packs(array, dim):
-    parts = lax.axis_size("dp")
-    shape = array.shape
-    cut = array.reshape(*shape[:dim], parts, shape[dim] // parts, *shape[dim + 1 :])
-    cut = jnp.moveaxis(cut, dim, 0)
-    arrived = lax.all_to_all(cut, "dp", split_axis=0, concat_axis=0, tiled=True)
-    return arrived.astype(jnp.float32).sum(axis=0)
 
 
 def shards(
@@ -316,7 +406,7 @@
     layer_output = (middle + matmul(hidden, down_whole)).astype(bf16)
 
     top_grad = output_grad.astype(jnp.float32)
-    grad_down = transposed_times(hidden, output_grad).astype(bf16)
+    grad_down = transposed_times(output_grad, hidden).astype(bf16)
     hidden_grad = times_transposed(output_grad, down_whole)
     pdf = jnp.exp(-0.5 * act * act) * (0.5 / jnp.pi) ** 0.5
     act_grad = (hidden_grad * lin * (cdf + act * pdf)).astype(bf16)
@@ -327,21 +417,22 @@
     middle_back, gain_mlp_part = norm_backward(mlp_norm_grad, normed_mlp, inv_mlp, mlp_gain)
     middle_grad = top_grad + middle_back
     attn_grad = middle_grad.astype(bf16)
-    grad_out = transposed_times(context, attn_grad).astype(bf16)
+    grad_out = transposed_times(attn_grad, context).astype(bf16)
+    half = D // 2
+    by_col = [
+        jnp.concatenate(
+            [g[:, c * (g.shape[1] // 2) : (c + 1) * (g.shape[1] // 2)] for g in grads], axis=1
+        )
+        for grads in [(grad_act, grad_lin, grad_down, grad_out)]
+        for c in range(2)
+    ]
+    stacked_grads = jnp.stack(by_col, axis=0).reshape(2, 2, half, -1).swapaxes(0, 1)
+    group_grads = kept_and_sent(kept_and_sent(stacked_grads, "row"), "col")
     context_grad = times_transposed(attn_grad, out_whole).astype(bf16)
     grad_own = swap_tokens_for_heads(context_grad)
 
     grad_heads = grad_own.reshape(total, own_heads, HEAD_DIM).transpose(1, 0, 2)
-    inner = jnp.sum(grad_heads.astype(jnp.float32) * context_heads, axis=2, keepdims=True)
-    ga = jnp.pad(
-        jnp.concatenate([grad_heads, three_parts(-inner)], axis=2),
-        ((0, 0), (0, 0), (0, LANES - HEAD_DIM - 3)),
-    )
-    minus_total = three_parts(-ctx[:, :, HEAD_DIM : HEAD_DIM + 1])
-    qa = jnp.concatenate(
-        [qa[:, :, : HEAD_DIM + 3], minus_total, qa[:, :, HEAD_DIM + 6 :]], axis=2
-    )
-    qkv_grad = attend_backward(qa, ka, va, ga, tables)
+    qkv_grad = attend_backward(qa, ka, va, grad_heads, ctx, tables)
 
     norm_partial = lax.dot_general(
         qkv_grad,
@@ -362,30 +453,39 @@
     stream_back, gain_attn_part = norm_backward(attn_norm_grad, normed_attn, inv_attn, attn_gain)
     grad_input = middle_grad + stream_back
 
-    def over_group(array, first, second):
-        array = lax.psum_scatter(array, first, scatter_dimension=0, tiled=True)
-        return lax.psum_scatter(array, second, scatter_dimension=1, tiled=True)
-
-    grad_out = sum_over_packs(over_group(grad_out, "col", "row"), 1)
-    grad_down = sum_over_packs(over_group(grad_down, "col", "row"), 1)
-    grad_act = sum_over_packs(over_group(grad_act, "row", "col"), 0)
-    grad_lin = sum_over_packs(over_group(grad_lin, "row", "col"), 0)
-    qkv_sums = sum_over_packs(attn_weight_grad, 0)
-    gains = lax.psum_scatter(
-        jnp.stack((gain_attn_part, gain_mlp_part), axis=1),
-        ("dp", "row", "col"),
-        scatter_dimension=0,
-        tiled=True,
+    peers = lax.axis_size("dp")
+    mine = jnp.concatenate([attn_weight_grad.reshape(half, -1), group_grads], axis=1)
+    summed = sum_over_packs(mine.reshape(peers, half // peers, -1), 0)
+    wide = 3 * half
+    qkv_sums = summed[:, :wide].reshape(-1, 3, half)
+    ff = act_weight.shape[1]
+    grad_act, grad_lin, grad_down = (
+        summed[:, wide + i * ff : wide + (i + 1) * ff] for i in range(3)
+    )
+    grad_out = summed[:, wide + 3 * ff :].T
+    grad_down = grad_down.T
+    devices = peers * 4
+    gain_parts = jnp.stack((gain_attn_part, gain_mlp_part), axis=0).reshape(2, devices, -1)
+    gains = (
+        lax.all_to_all(
+            gain_parts.swapaxes(0, 1).reshape(devices, -1),
+            ("dp", "row", "col"),
+            split_axis=0,
+            concat_axis=0,
+            tiled=True,
+        )
+        .sum(axis=0)
+        .reshape(2, -1)
     )
     return (
         layer_output,
         grad_input,
-        gains[:, 0],
+        gains[0],
         qkv_sums[:, 0],
         qkv_sums[:, 1],
         qkv_sums[:, 2],
         grad_out,
-        gains[:, 1],
+        gains[1],
         grad_act,
         grad_lin,
         grad_down,

time: 499 us -> 467 us (0.936)
  the two profiles are of different devices: /device:TPU:0 before, /device:TPU:11 now
where the time goes in v2:
time: 467 us; the launch traced here: 459 us
  Pallas kernels  165 us (35%)
  local copies, waits for them, and re-layouts  77 us (16%)
  waiting for transfers between devices  56.5 us (12%)
  matrix products  44.8 us (10%)
  blocking collectives  36.1 us (8%)
  starting transfers between devices  33.2 us (7%)
  other arithmetic  32.4 us (7%)
  between operations  14.5 us (3%)
    pallas_call x1, Pallas kernels, sum_over_packs(): pl.pallas_call(functools.partial(pack_sum_kernel, peers), in_specs=[vmem]...  62 us
    pallas_call x1, Pallas kernels, attend_backward(): pl.pallas_call(functools.partial(backward_kernel, rows), grid=(heads, tot...  61.4 us
    pallas_call x1, Pallas kernels, attend_forward(): pl.pallas_call(functools.partial(forward_kernel, rows), grid=(heads, tota...  41.2 us
    all_gather x4, blocking collectives, whole_weight(): weight = lax.all_gather(weight, second, axis=1, tiled=True)  36.1 us
    all_to_all x1, waiting for transfers between devices, shards(): lax.all_to_all(gain_parts.swapaxes(0, 1).reshape(devices, -1), ('dp', 'ro...  21.4 us
    all_to_all x1, waiting for transfers between devices, shards(): lax.all_to_all(norm_partial.reshape(4, quarter, D), ('row', 'col'), split...  16.8 us
    dot_general x4, matrix products, matmul(): return jnp.dot(left_side, right_side, preferred_element_type=jnp.float32)  15.3 us
    concatenate x2, local copies, waits for them, and re-layouts, shards(): jnp.concatenate([g[:, c * (g.shape[1] // 2):(c + 1) * (g.shape[1] // 2)]...  12.9 us
  transfers between devices with their start and end apart: 13, of which 4 were waited for; matrix products, arithmetic and copies ran while one was open for 26% of the time, Pallas kernels for 22%

profile of v2, /device:TPU:11, one launch (start us, length us, event | category | flops | bytes accessed | tf_op | source)
XLA Modules:
  0.0 459.0 jit_solution(559617262878211158)
XLA Ops:
  8.0 1.5 convert_reduce_fusion.1
  9.4 2.4 fusion.23
  11.9 2.7 all_gather.28
  14.7 15.5 %all_gather.30 = bf16[384,1152]{0,1:T(8,128)(2,1)} all-gather(bf16[384,576]{0,1:T(8,128)(2,1)S(1)} %copy-done.11), channel_id=1, replica_groups=mesh['dp'=8,'row'=2,'col'=2] {'col'}, dimensions={1}, use_global_device_ids=true | all-gather | bytes 1327104 | tf_op jit(solution)/shard_map/all_gather | solution.py:353
  30.3 2.0 copy.103
  32.3 6.5 %all-to-all-start = ((bf16[384,3,384]{0,1,2:T(4,128)(2,1)}), bf16[384,3,384]{0,1,2:T(4,128)(2,1)S(1)}, u32[]{:S(2)}, u32[]{:S(2)}) async-start(bf16[384,3,384]{0,1,2:T(4,128)(2,1)} %copy.103), calls=%async_computation | async-start | bytes 2359296 | tf_op jit(solution)/shard_map/all_to_all | solution.py:381
  38.9 15.1 %all_gather.32 = bf16[384,1152]{0,1:T(8,128)(2,1)} all-gather(bf16[384,576]{0,1:T(8,128)(2,1)S(1)} %copy-done.12), channel_id=1, replica_groups=mesh['dp'=8,'row'=2,'col'=2] {'col'}, dimensions={1}, use_global_device_ids=true | all-gather | bytes 1327104 | tf_op jit(solution)/shard_map/all_gather | solution.py:353
  55.9 2.5 copy.107.w_ref
  58.7 1.3 add_convert_fusion.1
  60.1 5.9 %fusion.31 = (f32[2048,128]{1,0:T(8,128)}, f32[2048,128]{1,0:T(8,128)}, f32[2048,128]{1,0:T(8,128)}) fusion(f32[128]{0:T(128)S(1)} %fusion.40, f32[2048]{0:T(1024)S(1)} %get-tuple-element.61, pred[128]{0:T(512)(128)(4,1)S(1)} %get-tuple-element.63, pred[128]{0:T(512)(128)(4,1)S(1)} %get-tuple-element.64), kind=kLoop, calls=%fused_computation.61 | loop fusion | flops 1048576 | bytes 3154688 | tf_op jit(solution)/shard_map/jit(_where)/select_n | solution.py:71
  65.9 41.2 %attend_forward.1 = (bf16[3,2048,128]{2,1,0:T(8,128)(2,1)}, bf16[3,2048,128]{2,1,0:T(8,128)(2,1)}, bf16[3,2048,128]{2,1,0:T(8,128)(2,1)}, f32[3,2048,128]{2,1,0:T(8,128)}) custom-call(bf16[2048,768]{1,0:T(8,128)(2,1)} %all-gather.6.cloned.1.call-done.h1_ref, bf16[3,768,384]{2,1,0:T(8,128)(2,1)} %copy.107.w_ref, f32[2048,128]{1,0:T(8,128)} %get-tuple-element.50.cos_ref, ...), custom_call_target="tpu_custom_call" | custom-call | flops 12884901888 | bytes 16777216 | tf_op jit(solution)/shard_map/attend_forward/pallas_call | solution.py:138
  107.1 2.1 fusion.30
  110.5 1.0 copy.109
  111.5 4.1 all-to-all-start.1
  115.6 2.9 all_gather.34
  118.6 7.8 %all-to-all-done.1 = bf16[4,512,192]{1,2,0:T(8,128)(2,1)S(1)} async-done(((bf16[4,512,192]{1,2,0:T(8,128)(2,1)}), bf16[4,512,192]{1,2,0:T(8,128)(2,1)S(1)}, u32[]{:S(2)}, u32[]{:S(2)}) %all-to-all-start.1) | async-done | bytes 786464 | tf_op jit(solution)/shard_map/all_to_all | solution.py:342
  126.5 2.4 fusion.41
  129.2 1.1 copy-done.9
  130.3 4.1 fusion.48
  134.4 4.5 fusion.49
  138.8 10.3 %all-gather.14.cloned.1.call-done = bf16[1152,768]{1,0:T(8,128)(2,1)} async-done(((bf16[576,768]{1,0:T(8,128)(2,1)}), bf16[1152,768]{1,0:T(8,128)(2,1)}) %all-gather.14.cloned.1.call-update) | async-done | bytes 1769488 | tf_op jit(solution)/shard_map/all_gather | solution.py:354
  149.1 5.0 %multiply_convert_fusion = (bf16[512,1152]{1,0:T(8,128)(2,1)S(1)}, bf16[512,1152]{1,0:T(8,128)(2,1)S(1)}, bf16[512,1152]{1,0:T(8,128)(2,1)}) fusion(f32[512,1152]{1,0:T(8,128)} %fusion.48, f32[512,1152]{1,0:T(8,128)} %fusion.49, bf16[512,768]{1,0:T(8,128)(2,1)S(1)} %copy-done.7, bf16[1152,768]{1,0:T(8,128)(2,1)} %all-gather.14.cloned.1.call-done), kind=kOutput, calls=%fused_computation.33 | convolution fusion | flops 915406848 | bytes 10813440 | tf_op jit(solution)/shard_map/dot_general | solution.py:26
  154.1 2.5 convolution_convert_fusion.2
  156.6 2.4 convolution_convert_fusion.1
  159.0 1.2 fusion.50
  160.5 1.6 multiply_reduce_fusion
  166.6 5.2 %all-to-all-start.2 = ((bf16[4,512,192]{1,2,0:T(8,128)(2,1)}), bf16[4,512,192]{1,2,0:T(8,128)(2,1)}, u32[]{:S(2)}, u32[]{:S(2)}) async-start(bf16[4,512,192]{1,2,0:T(8,128)(2,1)} %bitcast.16), calls=%async_computation.2 | async-start | bytes 1572864 | tf_op jit(solution)/shard_map/all_to_all | solution.py:335
  171.8 3.0 fusion.44
  174.9 1.4 fusion.43
  176.6 1.2 fusion.8
  177.9 1.8 fusion.42
  179.7 1.2 fusion.45
  180.8 6.3 %concatenate.17 = bf16[768,2112]{1,0:T(8,128)(2,1)} concatenate(bf16[768,576]{1,0:T(8,128)(2,1)S(1)} %get-tuple-element.39, bf16[768,576]{1,0:T(8,128)(2,1)S(1)} %get-tuple-element.37, bf16[768,576]{1,0:T(8,128)(2,1)} %get-tuple-element.35, bf16[768,384]{1,0:T(8,128)(2,1)} %get-tuple-element.41), dimensions={1} | concatenate | bytes 6488064 | tf_op jit(solution)/shard_map/concatenate | solution.py:423
  187.1 4.6 copy.125
  191.7 6.7 %concatenate.18 = bf16[768,2112]{1,0:T(8,128)(2,1)} concatenate(bf16[768,576]{1,0:T(8,128)(2,1)} %get-tuple-element.38, bf16[768,576]{1,0:T(8,128)(2,1)} %get-tuple-element.36, bf16[768,576]{1,0:T(8,128)(2,1)} %get-tuple-element.34, bf16[768,384]{1,0:T(8,128)(2,1)} %get-tuple-element.40), dimensions={1} | concatenate | bytes 6488064 | tf_op jit(solution)/shard_map/concatenate | solution.py:423
  198.4 5.4 %copy.126 = bf16[1,2,384,2112]{2,3,0,1:T(8,128)(2,1)} copy(bf16[1,2,384,2112]{3,2,1,0:T(8,128)(2,1)} %bitcast.104) | data formatting | bytes 6488064 | tf_op jit(solution)/shard_map/stack | solution.py:429
  203.8 3.6 fusion.2
  207.4 2.6 copy.113
  210.0 2.8 reshape_reshape.7
  212.8 2.5 copy.114
  215.3 61.4 %attend_backward.1 = bf16[3,2048,384]{2,1,0:T(8,128)(2,1)} custom-call(bf16[3,2048,128]{2,1,0:T(8,128)(2,1)} %get-tuple-element.16.qa_ref, bf16[3,2048,128]{2,1,0:T(8,128)(2,1)} %get-tuple-element.17.ka_ref, bf16[3,2048,128]{2,1,0:T(8,128)(2,1)} %get-tuple-element.18.va_ref, bf16[3,2048,64]{2,1,0:T(8,128)(2,1)} %bitcast.117, ...), custom_call_target="tpu_custom_call" | custom-call | flops 32212254720 | bytes 16777216 | tf_op jit(solution)/shard_map/attend_backward/pallas_call | solution.py:248
  276.7 6.2 %fusion.15 = bf16[768,3,384]{0,2,1:T(8,128)(2,1)S(1)} fusion(bf16[3,2048,384]{2,1,0:T(8,128)(2,1)} %attend_backward.1, bf16[2048,768]{1,0:T(8,128)(2,1)S(1)} %copy-done.20), kind=kOutput, calls=%fused_computation.36 | convolution fusion | flops 3624763392 | bytes 9633792 | tf_op jit(solution)/shard_map/dot_general | solution.py:447
  284.0 3.4 copy.120
  287.4 5.1 %all-to-all-start.5 = ((bf16[768,3,192]{2,1,0:T(4,128)(2,1)}), bf16[768,3,192]{2,1,0:T(4,128)(2,1)}, u32[]{:S(2)}, u32[]{:S(2)}) async-start(bf16[768,3,192]{2,1,0:T(4,128)(2,1)} %copy.120), calls=%async_computation.5 | async-start | bytes 3145728 | tf_op jit(solution)/shard_map/all_to_all | solution.py:452
  292.5 7.7 %bitcast_convert_fusion = bf16[2048,768]{1,0:T(8,128)(2,1)} fusion(bf16[3,2048,384]{2,1,0:T(8,128)(2,1)} %attend_backward.1, bf16[3,768,384]{1,2,0:T(8,128)(2,1)} %bitcast.106), kind=kOutput, calls=%fused_computation.6 | convolution fusion | flops 3625451520 | bytes 9633792 | tf_op jit(solution)/shard_map/dot_general | solution.py:437
  300.2 4.9 %all-to-all-start.3 = ((bf16[4,512,768]{2,1,0:T(8,128)(2,1)}), bf16[4,512,768]{2,1,0:T(8,128)(2,1)}, u32[]{:S(2)}, u32[]{:S(2)}) async-start(bf16[4,512,768]{2,1,0:T(8,128)(2,1)} %bitcast.114), calls=%async_computation.3 | async-start | bytes 6291456 | tf_op jit(solution)/shard_map/all_to_all | solution.py:443
  305.2 4.4 add_convert_fusion
  309.6 4.2 copy.143
  313.8 3.8 concatenate.16
  317.6 3.2 fusion
  320.9 1.5 dynamic-slice_bitcast_fusion
  323.1 1.4 collective-permute-start.1
  324.5 16.8 %all-to-all-done.3 = bf16[4,512,768]{2,1,0:T(8,128)(2,1)} async-done(((bf16[4,512,768]{2,1,0:T(8,128)(2,1)}), bf16[4,512,768]{2,1,0:T(8,128)(2,1)}, u32[]{:S(2)}, u32[]{:S(2)}) %all-to-all-start.3) | async-done | bytes 3145760 | tf_op jit(solution)/shard_map/all_to_all | solution.py:443
  341.3 2.5 convert_reduce_fusion
  343.8 2.0 fusion.28
  346.6 5.8 %all-to-all-start.4 = ((f32[32,1,48]{2,1,0:T(1,128)}), f32[32,1,48]{2,1,0:T(1,128)S(1)}, u32[]{:S(2)}, u32[]{:S(2)}) async-start(f32[32,1,48]{2,1,0:T(1,128)} %copy.117), calls=%async_computation.4 | async-start | bytes 32768 | tf_op jit(solution)/shard_map/all_to_all | solution.py:470
  352.5 2.8 fusion.27
  355.3 21.4 %all-to-all-done.4 = f32[32,1,48]{2,1,0:T(1,128)S(1)} async-done(((f32[32,1,48]{2,1,0:T(1,128)}), f32[32,1,48]{2,1,0:T(1,128)S(1)}, u32[]{:S(2)}, u32[]{:S(2)}) %all-to-all-start.4) | async-done | bytes 6176 | tf_op jit(solution)/shard_map/all_to_all | solution.py:470
  377.3 2.3 fusion.5
  379.6 1.2 copy.127
  380.8 2.8 pad_maximum_fusion.x_ref
  383.7 62.0 %sum_over_packs.1 = f32[48,3264]{1,0:T(8,128)} custom-call(bf16[8,48,3264]{2,1,0:T(8,128)(2,1)} %pad_maximum_fusion.x_ref), custom_call_target="tpu_custom_call" | custom-call | tf_op jit(solution)/shard_map/sum_over_packs/pallas_call | solution.py:303
  446.6 1.6 slice_bitcast_fusion.1
  448.3 1.8 slice_bitcast_fusion
  (113 shorter events, 16.4 us)
Async XLA Ops:
  7.2 4.7 %copy-start.14 = (bf16[384,384]{1,0:T(8,128)(2,1)S(1)}, bf16[384,384]{1,0:T(8,128)(2,1)}, u32[]{:S(2)}) copy-start(bf16[384,384]{1,0:T(8,128)(2,1)} %param.17) | copy-start | bytes 884740
  7.2 58.8 %all-gather.6.cloned.1.call-start = ((), (), s32[]{:S(2)}) async-start(), calls=%async_computation.6 | async-start | bytes 3932160 | tf_op jit(solution)/shard_map/all_gather | solution.py:349
  9.4 5.2 %copy-start.11 = (bf16[384,576]{0,1:T(8,128)(2,1)S(1)}, bf16[384,576]{0,1:T(8,128)(2,1)}, u32[]{:S(2)}) copy-start(bf16[384,576]{0,1:T(8,128)(2,1)} %param.19) | copy-start | bytes 1327108
  11.8 114.6 %all-gather.8.cloned.1.call-start = ((), (), s32[]{:S(2)}) async-start(), calls=%async_computation.7 | async-start | bytes 1769472 | tf_op jit(solution)/shard_map/all_gather | solution.py:354
  14.6 15.6 %copy-start.15 = (bf16[384,384]{1,0:T(8,128)(2,1)S(1)}, bf16[384,384]{1,0:T(8,128)(2,1)}, u32[]{:S(2)}) copy-start(bf16[384,384]{1,0:T(8,128)(2,1)} %param.16) | copy-start | bytes 884740
  14.6 15.6 %copy-start.16 = (bf16[384,384]{1,0:T(8,128)(2,1)S(1)}, bf16[384,384]{1,0:T(8,128)(2,1)}, u32[]{:S(2)}) copy-start(bf16[384,384]{1,0:T(8,128)(2,1)} %param.15) | copy-start | bytes 884740
  14.6 15.6 %copy-start.17 = (bf16[384,384]{1,0:T(8,128)(2,1)S(1)}, bf16[384,384]{1,0:T(8,128)(2,1)}, u32[]{:S(2)}) copy-start(bf16[384,384]{1,0:T(8,128)(2,1)} %param.14) | copy-start | bytes 884740
  14.6 114.6 %all-gather.10.cloned.1.call-start = ((), (), s32[]{:S(2)}) async-start(), calls=%async_computation.8 | async-start | bytes 2654208 | tf_op jit(solution)/shard_map/all_gather | solution.py:354
  32.3 6.5 %copy-start.12 = (bf16[384,576]{0,1:T(8,128)(2,1)S(1)}, bf16[384,576]{0,1:T(8,128)(2,1)}, u32[]{:S(2)}) copy-start(bf16[384,576]{0,1:T(8,128)(2,1)} %param.20) | copy-start | bytes 1327108
  32.3 21.7 %all-to-all-start = ((bf16[384,3,384]{0,1,2:T(4,128)(2,1)}), bf16[384,3,384]{0,1,2:T(4,128)(2,1)S(1)}, u32[]{:S(2)}, u32[]{:S(2)}) async-start(bf16[384,3,384]{0,1,2:T(4,128)(2,1)} %copy.103), calls=%async_computation | async-start | bytes 2359296 | tf_op jit(solution)/shard_map/all_to_all | solution.py:381
  38.9 95.5 %all-gather.12.cloned.1.call-start = ((), (), s32[]{:S(2)}) async-start(), calls=%async_computation.9 | async-start | bytes 2654208 | tf_op jit(solution)/shard_map/all_gather | solution.py:354
  55.9 2.5 copy-start.4
  55.9 2.5 copy-start.19
  110.5 5.1 %copy-start.13 = (bf16[576,384]{1,0:T(8,128)(2,1)S(1)}, bf16[576,384]{1,0:T(8,128)(2,1)}, u32[]{:S(2)}) copy-start(bf16[576,384]{1,0:T(8,128)(2,1)} %param.21) | copy-start | bytes 1327108
  111.5 7.0 %copy-start.18 = (bf16[768]{0:T(1024)(128)(2,1)S(1)}, bf16[768]{0:T(1024)(128)(2,1)}, u32[]{:S(2)}) copy-start(bf16[768]{0:T(1024)(128)(2,1)} %param.18) | copy-start | bytes 4612
  111.5 14.9 %all-to-all-start.1 = ((bf16[4,512,192]{1,2,0:T(8,128)(2,1)}), bf16[4,512,192]{1,2,0:T(8,128)(2,1)S(1)}, u32[]{:S(2)}, u32[]{:S(2)}) async-start(bf16[4,512,192]{1,2,0:T(8,128)(2,1)} %copy.109), calls=%async_computation.1 | async-start | bytes 1572864 | tf_op jit(solution)/shard_map/all_to_all | solution.py:342
  115.6 10.9 %copy-start.3 = (bf16[512,768]{1,0:T(8,128)(2,1)S(1)}, bf16[512,768]{1,0:T(8,128)(2,1)}, u32[]{:S(2)}) copy-start(bf16[512,768]{1,0:T(8,128)(2,1)} %param.12) | copy-start | bytes 2359300
  115.6 33.5 %all-gather.14.cloned.1.call-start = ((), (), s32[]{:S(2)}) async-start(), calls=%async_computation.10 | async-start | bytes 2654208 | tf_op jit(solution)/shard_map/all_gather | solution.py:354
  128.9 33.2 %copy-start.5 = (f32[512,768]{1,0:T(8,128)}, f32[512,768]{1,0:T(8,128)S(1)}, u32[]{:S(2)}) copy-start(f32[512,768]{1,0:T(8,128)S(1)} %get-tuple-element.59) | copy-start | bytes 4718596
  129.2 1.1 copy-start.9
  134.4 14.8 %copy-start.7 = (bf16[512,768]{1,0:T(8,128)(2,1)S(1)}, bf16[512,768]{1,0:T(8,128)(2,1)}, u32[]{:S(2)}) copy-start(bf16[512,768]{1,0:T(8,128)(2,1)} %param.23) | copy-start | bytes 2359300
  149.1 5.0 %copy-start.10 = (bf16[512,768]{1,0:T(8,128)(2,1)S(1)}, bf16[512,768]{1,0:T(8,128)(2,1)}, u32[]{:S(2)}) copy-start(bf16[512,768]{1,0:T(8,128)(2,1)} %copy-done.9) | copy-start | bytes 2359300
  156.6 2.4 copy-start.21
  159.0 1.5 copy-start.22
  162.7 1.2 copy-start
  162.7 1.8 copy-start.23
  166.6 40.8 %all-to-all-start.2 = ((bf16[4,512,192]{1,2,0:T(8,128)(2,1)}), bf16[4,512,192]{1,2,0:T(8,128)(2,1)}, u32[]{:S(2)}, u32[]{:S(2)}) async-start(bf16[4,512,192]{1,2,0:T(8,128)(2,1)} %bitcast.16), calls=%async_computation.2 | async-start | bytes 1572864 | tf_op jit(solution)/shard_map/all_to_all | solution.py:335
  171.8 3.1 copy-start.6
  174.9 1.4 copy-start.8
  174.9 1.7 copy-start.24
  207.4 110.3 %collective-permute-start = (bf16[2,384,2112]{1,2,0:T(8,128)(2,1)}, bf16[2,384,2112]{1,2,0:T(8,128)(2,1)}, u32[]{:S(2)}, u32[]{:S(2)}) collective-permute-start(bf16[2,384,2112]{1,2,0:T(8,128)(2,1)} %fusion.2), channel_id=1, source_target_pairs={{0,2},{2,0},{1,3},{3,1},{4,6},{6,4},{5,7},{7,5},{8,10},{10,8},{9,1... | collective-permute-start | bytes 9732104 | tf_op jit(solution)/shard_map/ppermute | solution.py:321
  215.3 61.4 %copy-start.20 = (bf16[2048,768]{1,0:T(8,128)(2,1)S(1)}, bf16[2048,768]{1,0:T(8,128)(2,1)}, u32[]{:S(2)}) copy-start(bf16[2048,768]{1,0:T(8,128)(2,1)} %all-gather.6.cloned.1.call-done.h1_ref) | copy-start | bytes 9437188
  287.4 12.8 %all-to-all-start.5 = ((bf16[768,3,192]{2,1,0:T(4,128)(2,1)}), bf16[768,3,192]{2,1,0:T(4,128)(2,1)}, u32[]{:S(2)}, u32[]{:S(2)}) async-start(bf16[768,3,192]{2,1,0:T(4,128)(2,1)} %copy.120), calls=%async_computation.5 | async-start | bytes 3145728 | tf_op jit(solution)/shard_map/all_to_all | solution.py:452
  300.2 41.0 %all-to-all-start.3 = ((bf16[4,512,768]{2,1,0:T(8,128)(2,1)}), bf16[4,512,768]{2,1,0:T(8,128)(2,1)}, u32[]{:S(2)}, u32[]{:S(2)}) async-start(bf16[4,512,768]{2,1,0:T(8,128)(2,1)} %bitcast.114), calls=%async_computation.3 | async-start | bytes 6291456 | tf_op jit(solution)/shard_map/all_to_all | solution.py:443
  320.8 2.2 copy-start.2
  323.1 54.2 %collective-permute-start.1 = (bf16[384,2112]{0,1:T(8,128)(2,1)}, bf16[384,2112]{0,1:T(8,128)(2,1)}, u32[]{:S(2)}, u32[]{:S(2)}) collective-permute-start(bf16[384,2112]{0,1:T(8,128)(2,1)} %dynamic-slice_bitcast_fusion), channel_id=1, source_target_pairs={{0,1},{1,0},{2,3},{3,2},{4,5},{5,4},{6,7},{7,6},{8,9},{9,8},{10,11... | collective-permute-start | bytes 4866056 | tf_op jit(solution)/shard_map/ppermute | solution.py:321
  343.8 8.7 %copy-start.1 = (f32[512,768]{1,0:T(8,128)S(1)}, f32[512,768]{1,0:T(8,128)}, u32[]{:S(2)}) copy-start(f32[512,768]{1,0:T(8,128)} %copy-done) | copy-start | bytes 4718596
  346.6 30.0 %all-to-all-start.4 = ((f32[32,1,48]{2,1,0:T(1,128)}), f32[32,1,48]{2,1,0:T(1,128)S(1)}, u32[]{:S(2)}, u32[]{:S(2)}) async-start(f32[32,1,48]{2,1,0:T(1,128)} %copy.117), calls=%async_computation.4 | async-start | bytes 32768 | tf_op jit(solution)/shard_map/all_to_all | solution.py:470
Sparse Core Ops, SparseCore 0:
  12.0 35.6 all-gather.5
  49.2 22.9 all-gather.7
  73.8 10.7 all-gather.9
  86.0 11.2 all-gather.11
  118.7 30.4 all-gather.13
